TPU v7x, 32 devices: a whole 2x2x4 slice. The times are simulated.
32 devices in a mesh: dp: 8 (over y, x, core), tensor: 4 (over z).
Axes of the slice: x: 2, y: 2, z: 4, core: 2. Of those that a mesh axis runs over, the one named last changes fastest.
Arguments:
- layer_input_rows: bfloat16 [512, 32, 768], P('tensor', 'dp'), may hold values from -6 to 6
- sentence_index_row: int32 [32, 512], P('dp'), may hold values from 0 to 7, as said below
- padding_mask: int32 [32, 512], P('dp'), may hold values from 0 to 1, as said below
- output_gradient: bfloat16 [512, 32, 768], P('tensor', 'dp'), may hold values from -6 to 6
- owner_rank: int32 [769], replicated, may hold values from 0 to 7, as said below
- master_state: float32 [4, 1536, 2304], P('tensor', 'dp'), may hold values from -1.5 to 1.5
- first_moment: float32 [4, 1536, 2304], P('tensor', 'dp')
- second_moment: float32 [4, 1536, 2304], P('tensor', 'dp'), as said below
Outputs:
- layer_out: float32 [512, 32, 768], P('tensor', 'dp')
- pooled_mean: float32 [32, 8, 768], P('dp', None, 'tensor')
- input_grad: float32 [512, 32, 768], P('tensor', 'dp')
- new_master: float32 [4, 1536, 2304], P('tensor', 'dp')
- new_first: float32 [4, 1536, 2304], P('tensor', 'dp')
- new_second: float32 [4, 1536, 2304], P('tensor', 'dp')
- norm_grads: float32 [6, 768], P(None, 'tensor')
Inputs may be any that keep to these rules, and one draw needn't show every extreme that they name: `owner_rank`: each dp index owns at most 192 blocks, and one of them owns exactly 192. `sentence_index_row`: ids never fall along a row; padding positions carry id 8 - 1 = 7. `padding_mask`: in every row the ones come first and cover at least 320 positions. `second_moment`: positive.
All inputs are finite; a program needn't handle non-finite values.
Results may differ from a plain program's by a relative error of at most 0.017.
Values may be sent and summed in bfloat16 or wider, within the bound.
A program may use at most 192 MiB of HBM per device.

v0:
```python
import jax
import functools
import jax.numpy as jnp
from jax import lax
from jax.experimental import pallas as pl
from jax.experimental.pallas import tpu as pltpu
from jax.sharding import PartitionSpec as P

MODEL_WIDTH = 768
HEAD_DIM = 64
FF = 3072
SMAX = 8
STEP = 10


NORM_EPS = 1e-05
ADAM_EPS = 1e-08
BETA_ONE = 0.9
BETA_TWO = 0.999
DECAY_RATE = 0.01
MASKED = -1e30
exact_precision = lax.Precision.HIGHEST


def slot_tables(owner_rank, per_owner):
    ordinal = jnp.arange(owner_rank.shape[0], dtype=jnp.int32)
    same_owner = owner_rank[:, None] == owner_rank[None, :]
    earlier = ordinal[None, :] < ordinal[:, None]
    ranking = jnp.sum((same_owner & earlier).astype(jnp.int32), axis=1)
    return owner_rank * per_owner + ranking


def slot_blocks(slot_of, wanted):
    matches = slot_of[None, :] == wanted[:, None]
    filled = jnp.any(matches, axis=1)
    ordinal = jnp.arange(slot_of.shape[0], dtype=jnp.int32)
    block_of = jnp.sum(jnp.where(matches, ordinal[None, :], 0), axis=1)
    return (block_of, filled)


def step_rates(token_position, width, hidden, tensor_size):
    width_loc = width // tensor_size
    ffn_loc = hidden // tensor_size
    end_up = width * ffn_loc
    end_down = end_up + ffn_loc * width
    end_qkv = end_down + width * 3 * width_loc
    end_out = end_qkv + width_loc * width
    offset = token_position - end_out
    first_gain = (offset >= 4 * width_loc + ffn_loc) & (offset < 5 * width_loc + ffn_loc)
    second_gain = (offset >= 6 * width_loc + ffn_loc) & (offset < 7 * width_loc + ffn_loc)
    small_rate = jnp.where(first_gain | second_gain, 0.2, 0.1)
    step_rate = jnp.where(
        token_position < end_up,
        width ** (-0.5),
        jnp.where(
            token_position < end_down,
            hidden ** (-0.5),
            jnp.where(
                token_position < end_qkv,
                width ** (-0.5),
                jnp.where(token_position < end_out, 4.0 * width ** (-0.5), small_rate),
            ),
        ),
    )
    decay_on = (token_position < end_out).astype(jnp.float32)
    return (step_rate.astype(jnp.float32), decay_on)


def adamw(gradient, moment, square, weight, step_rate, decay_on, filled):
    new_moment = BETA_ONE * moment + (1.0 - BETA_ONE) * gradient
    new_square = BETA_TWO * square + (1.0 - BETA_TWO) * gradient * gradient
    unbiased = new_moment / (1.0 - BETA_ONE**STEP)
    divisor = jnp.sqrt(new_square / (1.0 - BETA_TWO**STEP)) + ADAM_EPS
    new_weight = weight - step_rate * (unbiased / divisor + DECAY_RATE * decay_on * weight)
    zeroed = jnp.zeros_like(weight)
    return (
        jnp.where(filled, new_weight, zeroed),
        jnp.where(filled, new_moment, zeroed),
        jnp.where(filled, new_square, zeroed),
    )


def normalize(values):
    centred = values - jnp.mean(values, axis=-1, keepdims=True)
    inv_dev = lax.rsqrt(jnp.mean(centred * centred, axis=-1, keepdims=True) + NORM_EPS)
    return (centred * inv_dev, inv_dev)


def norm_back(grad_scaled, normed, inv_dev):
    first_mean = jnp.mean(grad_scaled, axis=-1, keepdims=True)
    second_mean = jnp.mean(grad_scaled * normed, axis=-1, keepdims=True)
    return inv_dev * (grad_scaled - first_mean - normed * second_mean)


def allowed_pairs(sentence_labels, real_token_flags):
    row_len = sentence_labels.shape[-1]
    same_sent = sentence_labels[:, :, None] == sentence_labels[:, None, :]
    live = (real_token_flags[:, :, None] == 1) & (real_token_flags[:, None, :] == 1)
    diagonal = jnp.eye(row_len, dtype=bool)[None]
    return same_sent & live | diagonal


def masked_scores(queries, key_rows, allowed, scaling):
    scores = (
        jnp.einsum("qshe,kshe->shqk", queries, key_rows, preferred_element_type=jnp.float32)
        * scaling
    )
    return jnp.where(allowed[:, None], scores, MASKED)


def split_flat(flat_all, width_loc, ffn_loc):
    end_up = MODEL_WIDTH * ffn_loc
    end_down = end_up + ffn_loc * MODEL_WIDTH
    end_qkv = end_down + MODEL_WIDTH * 3 * width_loc
    end_out = end_qkv + width_loc * MODEL_WIDTH
    return (
        flat_all[:end_up].reshape(MODEL_WIDTH, ffn_loc),
        flat_all[end_up:end_down].reshape(ffn_loc, MODEL_WIDTH),
        flat_all[end_down:end_qkv].reshape(MODEL_WIDTH, 3 * width_loc),
        flat_all[end_qkv:end_out].reshape(width_loc, MODEL_WIDTH),
        flat_all[end_out:],
    )


def local_general(
    layer_input_rows,
    sentence_index_row,
    padding_mask,
    output_gradient,
    owner_rank,
    master_state,
    first_moment,
    second_moment,
):
    tensor_size = lax.axis_size("tensor")
    tensor_at = lax.axis_index("tensor")
    data_size = lax.axis_size("dp")
    data_at = lax.axis_index("dp")
    width_loc = MODEL_WIDTH // tensor_size
    ffn_loc = FF // tensor_size
    heads_loc = width_loc // HEAD_DIM
    quarter = layer_input_rows.shape[0]
    seq_count = layer_input_rows.shape[1]
    row_len = quarter * tensor_size
    per_owner = master_state.shape[1]
    block_len = master_state.shape[2]
    nblocks = owner_rank.shape[0]
    slot_of = slot_tables(owner_rank, per_owner)
    gathered = lax.all_gather(master_state.astype(jnp.bfloat16), "dp", axis=1, tiled=True)[0]
    flat_weights = gathered[slot_of].reshape(nblocks * block_len)
    up_weight, down_weight, w_qkv, w_out, small_part = split_flat(flat_weights, width_loc, ffn_loc)
    bias_q = small_part[:width_loc].astype(jnp.float32)
    bias_v = small_part[width_loc : 2 * width_loc].astype(jnp.float32)
    expand_bias = small_part[2 * width_loc : 2 * width_loc + ffn_loc].astype(jnp.float32)
    norm_parts = small_part[2 * width_loc + ffn_loc :].reshape(6, width_loc)
    full_rows, norm_whole = (
        lax.all_gather(layer_input_rows, "tensor", axis=0, tiled=True),
        lax.all_gather(norm_parts, "tensor", axis=1, tiled=True),
    )
    norm_all = norm_whole.astype(jnp.float32)
    bias_out, bias_down = (norm_all[0], norm_all[1])
    gain_one, shift_one, gain_two, shift_two = (norm_all[2], norm_all[3], norm_all[4], norm_all[5])
    qkv_lin = jnp.einsum("lsd,de->lse", full_rows, w_qkv, preferred_element_type=jnp.float32)
    bias_qkv = jnp.concatenate([bias_q, jnp.zeros((width_loc,), jnp.float32), bias_v])
    qkv = (qkv_lin + bias_qkv).astype(jnp.bfloat16)
    queries = qkv[:, :, :width_loc].reshape(row_len, seq_count, heads_loc, HEAD_DIM)
    key_rows = qkv[:, :, width_loc : 2 * width_loc].reshape(row_len, seq_count, heads_loc, HEAD_DIM)
    values = qkv[:, :, 2 * width_loc :].reshape(row_len, seq_count, heads_loc, HEAD_DIM)
    scaling = HEAD_DIM ** (-0.5)
    allowed = allowed_pairs(sentence_index_row, padding_mask)
    scores = masked_scores(queries, key_rows, allowed, scaling)
    row_peak = jnp.max(scores, axis=-1, keepdims=True)
    log_total = row_peak + jnp.log(jnp.sum(jnp.exp(scores - row_peak), axis=-1, keepdims=True))
    prob_low = jnp.exp(scores - log_total).astype(jnp.bfloat16)
    attended = jnp.einsum("shqk,kshe->qshe", prob_low, values, preferred_element_type=jnp.float32)
    attended = attended.astype(jnp.bfloat16).reshape(row_len, seq_count, width_loc)
    portion_rows = attended
    attn_rows = lax.psum_scatter(
        jnp.einsum("lse,ed->lsd", portion_rows, w_out, preferred_element_type=jnp.float32).astype(
            jnp.bfloat16
        ),
        "tensor",
        scatter_dimension=0,
        tiled=True,
    ).astype(jnp.float32)
    z_one = layer_input_rows.astype(jnp.float32) + attn_rows + bias_out
    normed_one, inv_one = normalize(z_one)
    h_mine = normed_one * gain_one + shift_one
    hidden_narrow_whole = lax.all_gather(h_mine.astype(jnp.bfloat16), "tensor", axis=0, tiled=True)
    up_pre = (
        jnp.einsum(
            "wer,rb->web", hidden_narrow_whole, up_weight, preferred_element_type=jnp.float32
        )
        + expand_bias
    )
    activation_narrow = jax.nn.gelu(up_pre, approximate=False).astype(jnp.bfloat16)
    portion_rows = activation_narrow
    down_rows = lax.psum_scatter(
        jnp.einsum(
            "aij,jb->aib", portion_rows, down_weight, preferred_element_type=jnp.float32
        ).astype(jnp.bfloat16),
        "tensor",
        scatter_dimension=0,
        tiled=True,
    ).astype(jnp.float32)
    z_two = h_mine + down_rows + bias_down
    normed_two, inv_two = normalize(z_two)
    layer_out = normed_two * gain_two + shift_two
    seg_mine = lax.dynamic_slice_in_dim(sentence_index_row, tensor_at * quarter, quarter, 1)
    valid_mine = lax.dynamic_slice_in_dim(padding_mask, tensor_at * quarter, quarter, 1)
    sent_ids = jnp.arange(SMAX, dtype=jnp.int32)
    onehot_mine = (
        (seg_mine[:, :, None] == sent_ids[None, None, :]) & (valid_mine[:, :, None] == 1)
    ).astype(jnp.float32)
    pool_part = jnp.einsum("slc,lsd->scd", onehot_mine, layer_out, precision=exact_precision)
    onehot_full = (
        (sentence_index_row[:, :, None] == sent_ids[None, None, :])
        & (padding_mask[:, :, None] == 1)
    ).astype(jnp.float32)
    counts = jnp.sum(onehot_full, axis=1)
    grad_out = output_gradient.astype(jnp.float32) * valid_mine.T[:, :, None].astype(jnp.float32)
    d_gain_two = jnp.sum(grad_out * normed_two, axis=(0, 1))
    d_shift_two = jnp.sum(grad_out, axis=(0, 1))
    dz_two = norm_back(grad_out * gain_two, normed_two, inv_two)
    d_bias_down = jnp.sum(dz_two, axis=(0, 1))
    second_sum_gradient_wide = lax.all_gather(
        dz_two.astype(jnp.bfloat16), "tensor", axis=0, tiled=True
    )
    down_weight_gradient = jnp.einsum(
        "ipo,ipr->or",
        activation_narrow,
        second_sum_gradient_wide,
        preferred_element_type=jnp.float32,
    )
    activation_gradient = jnp.einsum(
        "ugp,jp->ugj", second_sum_gradient_wide, down_weight, preferred_element_type=jnp.float32
    )
    gelu_pull = jax.vjp(lambda pre_act: jax.nn.gelu(pre_act, approximate=False), up_pre)[1]
    d_up = gelu_pull(activation_gradient)[0]
    d_bias_up = jnp.sum(d_up, axis=(0, 1))
    expand_gradient_narrow = d_up.astype(jnp.bfloat16)
    up_weight_gradient = jnp.einsum(
        "iux,iuy->xy",
        hidden_narrow_whole,
        expand_gradient_narrow,
        preferred_element_type=jnp.float32,
    )
    portion_rows = expand_gradient_narrow
    dh_rows = lax.psum_scatter(
        jnp.einsum(
            "uih,vh->uiv", portion_rows, up_weight, preferred_element_type=jnp.float32
        ).astype(jnp.bfloat16),
        "tensor",
        scatter_dimension=0,
        tiled=True,
    ).astype(jnp.float32)
    dh_mine = dz_two + dh_rows
    d_gain_one = jnp.sum(dh_mine * normed_one, axis=(0, 1))
    d_shift_one = jnp.sum(dh_mine, axis=(0, 1))
    dz_one = norm_back(dh_mine * gain_one, normed_one, inv_one)
    d_bias_out = jnp.sum(dz_one, axis=(0, 1))
    dz_one_full = lax.all_gather(dz_one.astype(jnp.bfloat16), "tensor", axis=0, tiled=True)
    d_w_out = jnp.einsum("lse,lsd->ed", attended, dz_one_full, preferred_element_type=jnp.float32)
    d_attended = jnp.einsum("lsd,ed->lse", dz_one_full, w_out, preferred_element_type=jnp.float32)
    d_attended = d_attended.astype(jnp.bfloat16).reshape(row_len, seq_count, heads_loc, HEAD_DIM)
    scores_again = masked_scores(queries, key_rows, allowed, scaling)
    attn_prob = jnp.exp(scores_again - log_total)
    prob_again = attn_prob.astype(jnp.bfloat16)
    d_prob = jnp.einsum("qshe,kshe->shqk", d_attended, values, preferred_element_type=jnp.float32)
    d_values = jnp.einsum(
        "shqk,qshe->kshe", prob_again, d_attended, preferred_element_type=jnp.float32
    )
    inner = jnp.sum(d_prob * attn_prob, axis=-1, keepdims=True)
    d_scores = (attn_prob * (d_prob - inner)).astype(jnp.bfloat16)
    d_queries = (
        jnp.einsum("shqk,kshe->qshe", d_scores, key_rows, preferred_element_type=jnp.float32)
        * scaling
    )
    d_keys = (
        jnp.einsum("shqk,qshe->kshe", d_scores, queries, preferred_element_type=jnp.float32)
        * scaling
    )
    d_bias_q = jnp.sum(d_queries, axis=(0, 1)).reshape(width_loc)
    d_bias_v = jnp.sum(d_values, axis=(0, 1)).reshape(width_loc)
    d_qkv_low = jnp.concatenate(
        [
            d_queries.reshape(row_len, seq_count, width_loc),
            d_keys.reshape(row_len, seq_count, width_loc),
            d_values.reshape(row_len, seq_count, width_loc),
        ],
        axis=2,
    ).astype(jnp.bfloat16)
    d_w_qkv = jnp.einsum("lsd,lse->de", full_rows, d_qkv_low, preferred_element_type=jnp.float32)
    portion_rows = d_qkv_low
    dx_rows = lax.psum_scatter(
        jnp.einsum("lse,de->lsd", portion_rows, w_qkv, preferred_element_type=jnp.float32).astype(
            jnp.bfloat16
        ),
        "tensor",
        scatter_dimension=0,
        tiled=True,
    ).astype(jnp.float32)
    input_grad = dz_one + dx_rows
    shared_grads = jnp.stack(
        [d_bias_out, d_bias_down, d_gain_one, d_shift_one, d_gain_two, d_shift_two]
    )[None]
    pool_sum, shared_sum = (
        lax.psum_scatter(
            pool_part.astype(jnp.bfloat16), "tensor", scatter_dimension=2, tiled=True
        ).astype(jnp.float32),
        lax.psum_scatter(
            shared_grads.astype(jnp.bfloat16), "tensor", scatter_dimension=2, tiled=True
        ).astype(jnp.float32),
    )
    pooled_mean = pool_sum / jnp.maximum(counts, 1.0)[:, :, None]
    flat_grads = jnp.concatenate(
        [
            up_weight_gradient.reshape(-1),
            down_weight_gradient.reshape(-1),
            d_w_qkv.reshape(-1),
            d_w_out.reshape(-1),
            d_bias_q,
            d_bias_v,
            d_bias_up,
            shared_sum.reshape(-1),
        ]
    )
    grad_blocks = flat_grads.reshape(nblocks, block_len)
    wanted = data_at * per_owner + jnp.arange(per_owner, dtype=jnp.int32)
    block_of, filled = slot_blocks(slot_of, wanted)
    slot_grads = (
        jnp.zeros((data_size * per_owner, block_len), jnp.float32).at[slot_of].set(grad_blocks)
    )
    owned_grads = lax.psum_scatter(slot_grads, "dp", scatter_dimension=0, tiled=True)
    norm_grads = lax.psum(shared_sum[0], "dp")
    token_position = block_of[:, None] * block_len + jnp.arange(block_len, dtype=jnp.int32)[None, :]
    step_rate, decay_on = step_rates(token_position, MODEL_WIDTH, FF, tensor_size)
    new_master, new_first, new_second = adamw(
        owned_grads,
        first_moment[0],
        second_moment[0],
        master_state[0],
        step_rate,
        decay_on,
        filled[:, None],
    )
    return (
        layer_out,
        pooled_mean,
        input_grad,
        new_master[None],
        new_first[None],
        new_second[None],
        norm_grads,
    )


MESH = pl.DeviceIdType.MESH
BF = jnp.bfloat16
F32 = jnp.float32
WEIGHTS = ((576, 96), (768, 32), (768, 96), (768, 96))
MIB = 2**20


class Place:
    def __init__(self):
        d = lax.axis_index("dp")
        self.t = lax.axis_index("tensor")
        self.c = d % 2
        self.x = (d // 2) % 2
        self.y = d // 4
        self.xy = d // 2
        self.core = (d + 1 - 2 * self.c, self.t)
        self.right = (d + 2 - 4 * self.x, self.t)
        self.down = (d + 4 - 8 * self.y, self.t)
        self.diag = (d + 6 - 4 * self.x - 8 * self.y, self.t)
        self.deep = [None] + [(d, (self.t + k) % 4) for k in (1, 2, 3)]
        self.ahead = [(self.t + k) % 4 for k in range(4)]
        self.behind = [(self.t + 4 - k) % 4 for k in range(4)]

    def greet(self):
        barrier = pltpu.get_barrier_semaphore()
        peers = [self.core, self.right, self.down, self.diag] + self.deep[1:]
        for peer in peers:
            pl.semaphore_signal(barrier, inc=1, device_id=peer, device_id_type=MESH)
        pl.semaphore_wait(barrier, len(peers))


class Sender:
    def __init__(self, send_sems, recv_sems, local_sems):
        self.sems = (send_sems, recv_sems, local_sems)
        self.used = 0
        self.used_local = 0
        self.open = []

    def send(self, src, dst, peer):
        i = self.used
        self.used += 1
        copy = pltpu.make_async_remote_copy(
            src_ref=src,
            dst_ref=dst,
            send_sem=self.sems[0].at[i],
            recv_sem=self.sems[1].at[i],
            device_id=peer,
            device_id_type=MESH,
        )
        copy.start()
        self.open.append(copy)
        return copy

    def copy(self, src, dst):
        i = self.used_local
        self.used_local += 1
        copy = pltpu.make_async_copy(src, dst, self.sems[2].at[i])
        copy.start()
        return copy

    def finish(self):
        for copy in self.open:
            copy.wait_send()


def rows_of(place, rows, at=None):
    at = place.xy if at is None else at
    return pl.ds(pl.multiple_of(place.c * (4 * rows) + at * rows, 32), rows)


def half_of(place, rows):
    return pl.ds(pl.multiple_of(place.c * (4 * rows), 128), 4 * rows)


def interleave(size, parts):
    group = size // parts
    out_row = lax.broadcasted_iota(jnp.int32, (size, size), 0)
    col = lax.broadcasted_iota(jnp.int32, (size, size), 1)
    part = jnp.zeros((size, size), jnp.int32)
    for k in range(1, parts):
        part = part + (col >= k * group).astype(jnp.int32)
    return jnp.where(out_row == parts * (col - group * part) + part, 1.0, 0.0).astype(BF)


def interleave_out():
    out_row = lax.broadcasted_iota(jnp.int32, (32, 32), 0)
    col = lax.broadcasted_iota(jnp.int32, (32, 32), 1)
    part = (col >= 8).astype(jnp.int32) + (col >= 16).astype(jnp.int32)
    keep = (out_row == 3 * (col - 8 * part) + part) & (col < 24)
    return jnp.where(keep, 1.0, 0.0).astype(BF)


def dot_f32(a, b):
    return jnp.dot(a, b, preferred_element_type=F32)


def compact_out():
    out_row = lax.broadcasted_iota(jnp.int32, (192, 256), 0)
    col = lax.broadcasted_iota(jnp.int32, (192, 256), 1)
    group = jnp.zeros((192, 256), jnp.int32)
    for i in range(1, 8):
        group = group + (out_row >= 24 * i).astype(jnp.int32)
    return jnp.where(col == out_row + 8 * group, 1.0, 0.0).astype(BF)


def dot_nt(a, b):
    return lax.dot_general(a, b, (((1,), (1,)), ((), ())), preferred_element_type=F32)


def dot_tn(a, b):
    return lax.dot_general(a, b, (((0,), (0,)), ((), ())), preferred_element_type=F32)


def norm_vectors(small, norm):
    for i in range(6):
        at = 1152 + 192 * i
        norm[i : i + 1, :] = jnp.concatenate([small[t, 0:1, at : at + 192] for t in range(4)], axis=1)


def row_loop(body, step=128):
    @pl.loop(0, 512 // step)
    def _(i):
        body(pl.ds(pl.multiple_of(i * step, step), step))


def forward_kernel(
    master,
    slot_col,
    small_slot,
    id_col,
    id_row,
    x_in,
    gy_in,
    w_qkv,
    w_out,
    w_up,
    w_down,
    out_compact,
    small_out,
    x_out,
    gy_row,
    qkv_out,
    prob_out,
    att_out,
    n_one_out,
    h_out,
    act_out,
    pull_out,
    n_two_out,
    inv_out,
    row_out,
    pool_out,
    slots,
    canon,
    land,
    share,
    p_qkv,
    p_out,
    p_up,
    p_down,
    small_mine,
    small_land,
    small_total,
    small,
    norm,
    bias_qkv,
    v_qkv,
    v_out,
    v_compact,
    v_up,
    v_down,
    x_row,
    qkv,
    prob,
    att,
    n_one,
    h_wide,
    h_low,
    act,
    pull,
    total,
    inv,
    row_low,
    pool,
    send_sems,
    recv_sems,
    local_sems,
):
    place = Place()
    link = Sender(send_sems, recv_sems, local_sems)
    place.greet()
    whole = (w_qkv, w_out, w_up, w_down)
    held = (v_qkv, v_out, v_up, v_down)
    piece = (p_qkv, p_out, p_up, p_down)
    peers = (place.right, place.down, place.diag)
    mine_rows = pl.ds(pl.multiple_of(place.t * 128, 128), 128)
    tidy = []

    slots[place.c] = master[...].astype(BF)
    core_slots = link.send(slots.at[place.c], slots.at[place.c], place.core)
    x_moves = [
        link.send(x_in.at[place.ahead[k]], x_row.at[mine_rows], place.deep[k]) for k in (1, 2, 3)
    ]
    x_stay = link.copy(x_in.at[place.t], x_row.at[mine_rows])
    tidy.append(link.copy(gy_in.at[place.t], gy_row.at[mine_rows]))
    core_slots.wait_recv()

    pair_slots = slots[...].reshape(384, 2304)
    slot_id = lax.broadcasted_iota(jnp.int32, (96, 384), 1) + place.xy * 384
    shares = []
    order = [(1, place.right), (2, place.down), (3, place.diag), (0, None)]
    pick_small = jnp.where(small_slot[...] == slot_id[:8], 1.0, 0.0).astype(BF)
    small_mine[...] = dot_f32(pick_small, pair_slots)
    small_moves = [link.send(small_mine, small_land.at[j], peer) for j, peer in enumerate(peers)]
    for j, peer in order:
        at = place.xy if peer is None else peer[0] // 2
        wanted = slot_col[pl.ds(pl.multiple_of(at * 96, 96), 96), :]
        pick = jnp.where(wanted == slot_id, 1.0, 0.0).astype(BF)
        canon[j] = dot_f32(pick, pair_slots).astype(BF)
        if peer is not None:
            shares.append(link.send(canon.at[j], land.at[j - 1], peer))
    for move in shares + small_moves:
        move.wait_recv()
    share[...] = (
        canon[0].astype(F32) + land[0].astype(F32) + land[1].astype(F32) + land[2].astype(F32)
    )
    small_total[...] = small_mine[...] + small_land[0] + small_land[1] + small_land[2]

    three = interleave(96, 3)
    p_qkv[...] = dot_f32(
        interleave(96, 4),
        jnp.concatenate([share[64:88, 576 * r : 576 * r + 576] for r in range(4)], axis=0).astype(BF),
    ).astype(BF)
    out_parts = [share[88:96, 768 * k : 768 * k + 768] for k in range(3)]
    out_parts = out_parts + [jnp.zeros((8, 768), F32)]
    p_out[...] = dot_f32(interleave_out(), jnp.concatenate(out_parts, axis=0).astype(BF)).astype(BF)

    def spread_ffn():
        for at, ref in ((0, p_up), (32, p_down)):
            parts = [share[at : at + 32, 768 * k : 768 * k + 768] for k in range(3)]
            ref[...] = dot_f32(three, jnp.concatenate(parts, axis=0).astype(BF)).astype(BF)

    deep_moves, right_moves, down_moves, own_copies, core_moves, loads = {}, {}, {}, {}, {}, {}

    def deep_send(w):
        spot = whole[w].at[place.t, rows_of(place, WEIGHTS[w][1])]
        own_copies[w] = link.copy(piece[w], spot)
        deep_moves[w] = [link.send(piece[w], spot, place.deep[k]) for k in (1, 2, 3)]

    def plane_send(w, k):
        rows = WEIGHTS[w][1]
        spot = whole[w].at[place.behind[k], rows_of(place, rows)]
        src = piece[w] if k == 0 else spot
        if k:
            deep_moves[w][k - 1].wait_recv()
        right_moves[w, k] = link.send(src, spot, place.right)
        down_moves[w, k] = link.send(src, spot, place.down)

    def plane_pass(w, k):
        rows = WEIGHTS[w][1]
        half = rows // 2
        right_moves[w, k].wait_recv()
        down_moves[w, k].wait_recv()
        t = place.behind[k]
        right_at = place.c * (4 * rows) + (place.right[0] // 2) * rows
        down_at = place.c * (4 * rows) + (place.down[0] // 2) * rows
        first = whole[w].at[t, pl.ds(pl.multiple_of(right_at, 16), half)]
        second = whole[w].at[t, pl.ds(pl.multiple_of(down_at + half, 16), half)]
        right_moves[w, k, 1] = link.send(second, second, place.right)
        down_moves[w, k, 1] = link.send(first, first, place.down)

    def core_pass(w, k):
        if k == 0:
            own_copies[w].wait()
        right_moves[w, k, 1].wait_recv()
        down_moves[w, k, 1].wait_recv()
        spot = whole[w].at[place.behind[k], half_of(place, WEIGHTS[w][1])]
        core_moves[w, k] = link.send(spot, spot, place.core)

    def load(w, k):
        core_moves[w, k].wait_recv()
        t = place.behind[k]
        loads[w, k] = link.copy(whole[w].at[t], held[w].at[t])

    def qkv_step(k):
        loads[0, k].wait()
        t = place.behind[k]

        def body(rows):
            lin = dot_f32(x_row[rows, :], v_qkv[t]) + bias_qkv[t]
            qkv[t, rows, :] = lin.astype(BF)

        row_loop(body)

    def attention(t):
        def body(rows):
            allowed = id_col[rows, :] == id_row[...]
            parts = []
            for i in range(3):
                at = 64 * i
                scores = dot_nt(qkv[t, rows, at : at + 64], qkv[t, :, 192 + at : 256 + at]) * 0.125
                scores = jnp.where(allowed, scores, MASKED)
                weight = jnp.exp(scores - jnp.max(scores, axis=1, keepdims=True))
                weight = weight * (1.0 / jnp.sum(weight, axis=1, keepdims=True))
                low = weight.astype(BF)
                prob[3 * t + i, rows, :] = low
                parts.append(dot_f32(low, qkv[t, :, 384 + at : 448 + at]))
            att[t, rows, :] = jnp.concatenate(parts, axis=1).astype(BF)

        row_loop(body)
        tidy.append(link.copy(qkv.at[t], qkv_out.at[t]))
        tidy.append(link.copy(att.at[t], att_out.at[t]))
        tidy.append(link.copy(prob.at[pl.ds(3 * t, 3)], prob_out.at[pl.ds(3 * t, 3)]))

    def out_step():
        pick = compact_out()
        for k in range(4):
            loads[1, k].wait()
        for t in range(4):
            v_compact[t] = dot_f32(pick, v_out[t]).astype(BF)
        tidy.append(link.copy(v_compact, out_compact))

        def body(rows):
            z = x_row[rows, :].astype(F32) + norm[0:1, :]
            for t in range(4):
                z = z + dot_f32(att[t, rows, :], v_compact[t])
            normed, inverse = normalize(z)
            n_one[rows, :] = normed
            inv[0, rows, :] = inverse
            h = normed * norm[2:3, :] + norm[3:4, :]
            h_low[rows, :] = h.astype(BF)
            h_wide[rows, :] = h
            total[rows, :] = h + norm[1:2, :]

        row_loop(body)
        tidy.append(link.copy(n_one, n_one_out))
        tidy.append(link.copy(h_low, h_out))

    def up_step(k):
        loads[2, k].wait()
        t = place.behind[k]

        def body(rows):
            pre = dot_f32(h_low[rows, :], v_up[t]) + small[t, 0:1, 384:1152]
            below = 0.5 + 0.5 * lax.erf(pre * (0.5**0.5))
            act[t, rows, :] = (pre * below).astype(BF)
            slope = below + pre * (jnp.exp(-0.5 * pre * pre) * 0.3989422804014327)
            pull[t, rows, :] = slope.astype(BF)

        row_loop(body)
        tidy.append(link.copy(act.at[t], act_out.at[t]))
        tidy.append(link.copy(pull.at[t], pull_out.at[t]))

    def down_step(k):
        loads[3, k].wait()
        t = place.behind[k]

        def body(rows):
            total[rows, :] += dot_f32(act[t, rows, :], v_down[t])

        row_loop(body)

    def end_step():
        ids = lax.broadcasted_iota(jnp.int32, (SMAX, 512), 0)
        member = jnp.where(ids == id_row[...], 1.0, 0.0)
        count = jnp.maximum(jnp.sum(member, axis=1, keepdims=True), 1.0)

        def body(rows):
            normed, inverse = normalize(total[rows, :])
            inv[1, rows, :] = inverse
            out = normed * norm[4:5, :] + norm[5:6, :]
            total[rows, :] = normed
            h_wide[rows, :] = out
            row_low[rows, :] = out.astype(BF)

        row_loop(body)
        pool[...] = jnp.dot(member, h_wide[...], precision=exact_precision, preferred_element_type=F32) / count
        tidy.append(link.copy(total, n_two_out))
        tidy.append(link.copy(row_low, row_out))
        tidy.append(link.copy(pool, pool_out))
        tidy.append(link.copy(inv, inv_out))

    every = range(4)
    deep_send(0)
    deep_send(1)
    tidy.append(link.copy(small_total, small.at[place.t]))
    small_deep = [link.send(small_total, small.at[place.t], place.deep[k]) for k in (1, 2, 3)]
    plane_send(0, 0)
    plane_send(1, 0)
    spread_ffn()
    plane_send(2, 0)
    for k in (1, 2, 3):
        plane_send(0, k)
    deep_send(2)
    plane_send(3, 0)
    for k in every:
        plane_pass(0, k)
    for k in (1, 2, 3):
        plane_send(1, k)
    for move in small_deep:
        move.wait_recv()
    tidy.pop().wait()
    norm_vectors(small, norm)
    for t in every:
        bias_qkv[t] = jnp.concatenate(
            [small[t, 0:1, :192], jnp.zeros((1, 192), F32), small[t, 0:1, 192:384]], axis=1
        )
    tidy.append(link.copy(small, small_out))
    x_stay.wait()
    for move in x_moves:
        move.wait_recv()
    tidy.append(link.copy(x_row, x_out))
    for k in every:
        core_pass(0, k)
    for k in every:
        plane_pass(1, k)
    for k in every:
        load(0, k)
    for k in (1, 2, 3):
        plane_send(2, k)
    deep_send(3)
    gy_moves = [
        link.send(gy_in.at[place.ahead[k]], gy_row.at[mine_rows], place.deep[k]) for k in (1, 2, 3)
    ]
    for k in every:
        qkv_step(k)
    for k in every:
        core_pass(1, k)
    plane_pass(2, 0)
    plane_pass(2, 1)
    for k in every:
        load(1, k)
    attention(0)
    plane_pass(2, 2)
    plane_pass(2, 3)
    for k in (1, 2, 3):
        plane_send(3, k)
    attention(1)
    for k in every:
        core_pass(2, k)
    attention(2)
    for k in every:
        load(2, k)
    plane_pass(3, 0)
    attention(3)
    plane_pass(3, 1)
    out_step()
    plane_pass(3, 2)
    plane_pass(3, 3)
    core_pass(3, 0)
    up_step(0)
    core_pass(3, 1)
    load(3, 0)
    up_step(1)
    core_pass(3, 2)
    core_pass(3, 3)
    up_step(2)
    load(3, 1)
    up_step(3)
    load(3, 2)
    load(3, 3)
    for k in every:
        down_step(k)
    end_step()
    for move in gy_moves:
        move.wait_recv()
    for copy in tidy:
        copy.wait()
    link.finish()


def forward_call(master, slot_col, small_slot, id_col, id_row, x_in, gy_in):
    anywhere = pl.BlockSpec(memory_space=pl.ANY)
    vmem = pl.BlockSpec(memory_space=pltpu.VMEM)
    shape = jax.ShapeDtypeStruct
    outs = [
        ((4, 768, 576), BF),
        ((4, 256, 768), BF),
        ((4, 768, 768), BF),
        ((4, 768, 768), BF),
        ((4, 192, 768), BF),
        ((4, 8, 2304), F32),
        ((512, 768), BF),
        ((512, 768), BF),
        ((4, 512, 576), BF),
        ((12, 512, 512), BF),
        ((4, 512, 192), BF),
        ((512, 768), F32),
        ((512, 768), BF),
        ((4, 512, 768), BF),
        ((4, 512, 768), BF),
        ((512, 768), F32),
        ((2, 512, 1), F32),
        ((512, 768), BF),
        ((8, 768), F32),
    ]
    scratch = [
        ((2, 192, 2304), BF),
        ((4, 96, 2304), BF),
        ((3, 96, 2304), BF),
        ((96, 2304), F32),
        ((96, 576), BF),
        ((32, 768), BF),
        ((96, 768), BF),
        ((96, 768), BF),
        ((8, 2304), F32),
        ((3, 8, 2304), F32),
        ((8, 2304), F32),
        ((4, 8, 2304), F32),
        ((8, 768), F32),
        ((4, 1, 576), F32),
        ((4, 768, 576), BF),
        ((4, 256, 768), BF),
        ((4, 192, 768), BF),
        ((4, 768, 768), BF),
        ((4, 768, 768), BF),
        ((512, 768), BF),
        ((4, 512, 576), BF),
        ((12, 512, 512), BF),
        ((4, 512, 192), BF),
        ((512, 768), F32),
        ((512, 768), F32),
        ((512, 768), BF),
        ((4, 512, 768), BF),
        ((4, 512, 768), BF),
        ((512, 768), F32),
        ((2, 512, 1), F32),
        ((512, 768), BF),
        ((8, 768), F32),
    ]
    return pl.pallas_call(
        forward_kernel,
        out_shape=[shape(*o) for o in outs],
        in_specs=[vmem] * 5 + [anywhere] * 2,
        out_specs=[anywhere] * len(outs),
        scratch_shapes=[pltpu.VMEM(*s) for s in scratch]
        + [
            pltpu.SemaphoreType.DMA((112,)),
            pltpu.SemaphoreType.DMA((112,)),
            pltpu.SemaphoreType.DMA((64,)),
        ],
        compiler_params=pltpu.CompilerParams(
            collective_id=0, has_side_effects=True, vmem_limit_bytes=60 * MIB
        ),
        name="gather_and_forward",
    )(master, slot_col, small_slot, id_col, id_row, x_in, gy_in)


def add_into(total, other, rows, step):
    groups = other.shape[0]

    @pl.loop(0, groups * (rows // step))
    def _(i):
        g = i // (rows // step)
        at = pl.ds(pl.multiple_of((i % (rows // step)) * step, step), step)
        total[g, at, :] = total[g, at, :] + other[g, at, :]


def reduce_kernel(
    g_qkv,
    g_out,
    g_up,
    g_down,
    small_in,
    out_row,
    dx_row,
    pool_in,
    blocks,
    small_out,
    out_mine,
    dx_mine,
    pool_out,
    *scratch,
):
    sums, cores, lefts, tops, lefts_two, tops_two, deeps = (scratch[4 * i : 4 * i + 4] for i in range(7))
    share, share_low, small_sum, small_land, send_sems, recv_sems, local_sems = scratch[28:]
    place = Place()
    link = Sender(send_sems, recv_sems, local_sems)
    grads = (g_qkv, g_out, g_up, g_down)
    loads = {}
    order = (3, 2, 1, 0)
    for w in order:
        rows = WEIGHTS[w][1]
        loads[w] = link.copy(grads[w].at[:, half_of(place, rows)], sums[w])
    place.greet()
    t, x, y = place.t, place.x, place.y
    core_moves = {}
    for w in order:
        rows = WEIGHTS[w][1]
        other = pl.ds(pl.multiple_of((1 - place.c) * (4 * rows), 128), 4 * rows)
        core_moves[w] = link.send(grads[w].at[:, other], cores[w], place.core)
    moves = []
    stay = [link.copy(small_in.at[t], small_sum.at[pl.ds(0, 1)])]
    small_moves = [link.send(small_in.at[place.ahead[k]], small_land.at[k - 1], place.deep[k]) for k in (1, 2, 3)]
    for src, dst in ((out_row, out_mine), (dx_row, dx_mine)):
        stay.append(link.copy(src.at[pl.ds(pl.multiple_of(t * 128, 128), 128)], dst.at[t]))
        for k in (1, 2, 3):
            part = src.at[pl.ds(pl.multiple_of(place.ahead[k] * 128, 128), 128)]
            moves.append(link.send(part, dst.at[t], place.deep[k]))
    stay.append(link.copy(pool_in, pool_out.at[t]))
    for k in (1, 2, 3):
        moves.append(link.send(pool_in, pool_out.at[t], place.deep[k]))

    first, second, third = {}, {}, {}

    def chip_row(w, yy, xx, half):
        rows = WEIGHTS[w][1]
        at = pl.multiple_of((yy * 2 + xx) * rows + half * (rows // 2), 16)
        return sums[w].at[:, pl.ds(at, rows // 2)]

    def add(total, other):
        groups, rows, _ = other.shape
        add_into(total, other, rows, 16)

    def stage_core(w):
        loads[w].wait()
        core_moves[w].wait_recv()
        add_into(sums[w], cores[w], 4 * WEIGHTS[w][1], 32)
        first[w] = []
        for i in (0, 1):
            first[w].append(link.send(chip_row(w, i, 1 - x, 0), lefts[w].at[i], place.right))
            first[w].append(link.send(chip_row(w, 1 - y, i, 1), tops[w].at[i], place.down))

    def stage_plane(w):
        for move in first[w]:
            move.wait_recv()
        add(chip_row(w, 1 - y, x, 0), lefts[w].at[1 - y])
        add(chip_row(w, y, 1 - x, 1), tops[w].at[1 - x])
        second[w] = [
            link.send(chip_row(w, 1 - y, x, 0), lefts_two[w], place.down),
            link.send(chip_row(w, y, 1 - x, 1), tops_two[w], place.right),
        ]
        add(chip_row(w, y, x, 0), lefts[w].at[y])
        add(chip_row(w, y, x, 1), tops[w].at[x])

    def stage_deep(w):
        for move in second[w]:
            move.wait_recv()
        add(chip_row(w, y, x, 0), lefts_two[w])
        add(chip_row(w, y, x, 1), tops_two[w])
        rows = WEIGHTS[w][1]
        spot = pl.ds(pl.multiple_of(place.xy * rows, 16), rows)
        third[w] = [
            link.send(sums[w].at[place.ahead[k], spot], deeps[w].at[k - 1], place.deep[k])
            for k in (1, 2, 3)
        ]

    def stage_end(w):
        for move in third[w]:
            move.wait_recv()
        rows = WEIGHTS[w][1]
        spot = pl.ds(pl.multiple_of(place.xy * rows, 16), rows)
        total = sums[w][t, spot, :].astype(F32)
        for k in range(3):
            total = total + deeps[w][k].astype(F32)
        total = total.astype(BF)
        turned = (((0,), (0,)), ((), ()))
        if w == 0:
            parts = lax.dot_general(interleave(96, 4), total, turned, preferred_element_type=F32)
            share[64:88, :] = jnp.concatenate([parts[24 * r : 24 * r + 24] for r in range(4)], axis=1)
        elif w == 1:
            parts = lax.dot_general(interleave_out(), total, turned, preferred_element_type=F32)
            for k in range(3):
                share[88:96, 768 * k : 768 * k + 768] = parts[8 * k : 8 * k + 8]
        else:
            at = 0 if w == 2 else 32
            parts = lax.dot_general(interleave(96, 3), total, turned, preferred_element_type=F32)
            for k in range(3):
                share[at : at + 32, 768 * k : 768 * k + 768] = parts[32 * k : 32 * k + 32]

    stage_core(3)
    stage_core(2)
    stage_plane(3)
    stage_core(1)
    stage_core(0)
    stage_deep(3)
    stage_plane(2)
    stage_plane(1)
    stage_deep(2)
    stage_plane(0)
    stage_end(3)
    stage_deep(1)

    stay[0].wait()
    for move in small_moves:
        move.wait_recv()
    small_sum[0] = (
        small_sum[0] + small_land[0, 0] + small_land[1, 0] + small_land[2, 0]
    )
    stage_end(2)
    stage_deep(0)
    stage_end(1)
    for i, peer in enumerate((place.core, place.right, place.down)):
        move = link.send(
            small_sum.at[pl.ds(i, 1)], small_land.at[3 + i], peer
        )
        move.wait_recv()
        small_sum[i + 1] = small_sum[i] + small_land[3 + i, 0]
    stage_end(0)
    small_out[...] = small_sum[3]

    share_low[...] = share[...].astype(BF)
    dest = pl.ds(pl.multiple_of((place.c * 4 + place.xy) * 96, 96), 96)
    keep = link.copy(share_low, blocks.at[dest])
    last = [link.send(share_low, blocks.at[dest], peer) for peer in (place.diag, place.right, place.down)]
    keep.wait()
    for move in last:
        move.wait_recv()
    half = pl.ds(pl.multiple_of(place.c * 384, 384), 384)
    across = link.send(blocks.at[half], blocks.at[half], place.core)
    across.wait_recv()
    for move in moves:
        move.wait_recv()
    for copy in stay[1:]:
        copy.wait()
    link.finish()


def reduce_call(g_qkv, g_out, g_up, g_down, small_in, out_row, dx_row, pool_in):
    anywhere = pl.BlockSpec(memory_space=pl.ANY)
    vmem = pl.BlockSpec(memory_space=pltpu.VMEM)
    shape = jax.ShapeDtypeStruct
    sums = [pltpu.VMEM((4, 4 * rows, cols), BF) for cols, rows in WEIGHTS]
    halves = [pltpu.VMEM((2, 4, rows // 2, cols), BF) for cols, rows in WEIGHTS]
    singles = [pltpu.VMEM((4, rows // 2, cols), BF) for cols, rows in WEIGHTS]
    deeps = [pltpu.VMEM((3, rows, cols), BF) for cols, rows in WEIGHTS]
    return pl.pallas_call(
        reduce_kernel,
        out_shape=[
            shape((768, 2304), BF),
            shape((24, 128), F32),
            shape((4, 128, 768), BF),
            shape((4, 128, 768), BF),
            shape((4, 8, 768), F32),
        ],
        in_specs=[anywhere] * 8,
        out_specs=[anywhere, vmem, anywhere, anywhere, anywhere],
        scratch_shapes=sums
        + sums
        + halves
        + halves
        + singles
        + singles
        + deeps
        + [
            pltpu.VMEM((96, 2304), F32),
            pltpu.VMEM((96, 2304), BF),
            pltpu.VMEM((4, 24, 128), F32),
            pltpu.VMEM((6, 1, 24, 128), F32),
            pltpu.SemaphoreType.DMA((80,)),
            pltpu.SemaphoreType.DMA((80,)),
            pltpu.SemaphoreType.DMA((12,)),
        ],
        compiler_params=pltpu.CompilerParams(
            collective_id=1, has_side_effects=True, vmem_limit_bytes=56 * MIB
        ),
        name="reduce_gradients",
    )(g_qkv, g_out, g_up, g_down, small_in, out_row, dx_row, pool_in)


def local_rows(
    layer_input_rows,
    sentence_index_row,
    padding_mask,
    output_gradient,
    owner_rank,
    master_state,
    first_moment,
    second_moment,
):
    tensor_at = lax.axis_index("tensor")
    data_at = lax.axis_index("dp")
    per_owner = master_state.shape[1]
    block_len = master_state.shape[2]
    slot_of = slot_tables(owner_rank, per_owner)
    slot_order = jnp.concatenate(
        [
            slot_of[:256].reshape(2, 4, 32),
            slot_of[256:512].reshape(2, 4, 32),
            slot_of[512:704].reshape(2, 4, 24),
            slot_of[704:768].reshape(2, 4, 8),
        ],
        axis=2,
    ).reshape(768)
    core_order = lax.dynamic_slice_in_dim(slot_order, (data_at % 2) * 384, 384, 0)[:, None]
    small_slot = jnp.broadcast_to(slot_of[768], (8, 1))

    labels = lax.dynamic_index_in_dim(sentence_index_row, tensor_at, 0, keepdims=False)
    flags = lax.dynamic_index_in_dim(padding_mask, tensor_at, 0, keepdims=False)
    ids = jnp.where(flags == 1, labels, -1 - jnp.arange(flags.shape[0], dtype=jnp.int32))
    (
        w_qkv,
        _,
        w_up,
        w_down,
        w_out,
        small_all,
        x_row,
        gy_row,
        qkv,
        prob_low,
        attended,
        normed_one,
        h_low,
        act,
        pull,
        normed_two,
        inverse,
        out_row,
        pool_mean,
    ) = forward_call(
        master_state[0],
        core_order,
        small_slot,
        ids[:, None],
        ids[None],
        jnp.transpose(layer_input_rows, (1, 0, 2)),
        jnp.transpose(output_gradient, (1, 0, 2)),
    )
    norm_all = small_all[:, 0, 1152:].reshape(4, 6, 192).transpose(1, 0, 2).reshape(6, 768)
    gain_one, gain_two = norm_all[2], norm_all[4]
    qkv = qkv.reshape(4, 512, 3, 3, HEAD_DIM)
    queries, keys, values = (qkv[:, :, i] for i in range(3))
    scaling = HEAD_DIM ** (-0.5)
    prob_low = prob_low.reshape(4, 3, 512, 512)
    attn_prob = prob_low.astype(F32)
    inv_one, inv_two = inverse[0], inverse[1]
    w_out = w_out.reshape(768, 768)
    attended = attended.transpose(1, 0, 2).reshape(512, 768)

    grad_out = gy_row.astype(F32) * flags[:, None].astype(F32)
    d_gain_two = jnp.sum(grad_out * normed_two, axis=0)
    d_shift_two = jnp.sum(grad_out, axis=0)
    dz_two = norm_back(grad_out * gain_two, normed_two, inv_two)
    d_bias_down = jnp.sum(dz_two, axis=0)
    dz_two_low = dz_two.astype(BF)
    g_down = jnp.einsum("tlf,ld->tfd", act, dz_two_low, preferred_element_type=F32).astype(BF)
    d_act = jnp.einsum("ld,tfd->tlf", dz_two_low, w_down, preferred_element_type=F32)
    d_up = d_act * pull.astype(F32)
    d_bias_up = jnp.sum(d_up, axis=1)
    d_up_low = d_up.astype(BF)
    g_up = jnp.einsum("ld,tlf->tdf", h_low, d_up_low, preferred_element_type=F32).astype(BF)
    dh = dz_two + jnp.einsum("tlf,tdf->ld", d_up_low, w_up, preferred_element_type=F32)
    d_gain_one = jnp.sum(dh * normed_one, axis=0)
    d_shift_one = jnp.sum(dh, axis=0)
    dz_one = norm_back(dh * gain_one, normed_one, inv_one)
    d_bias_out = jnp.sum(dz_one, axis=0)
    dz_one_low = dz_one.astype(BF)
    g_out = jnp.einsum("le,ld->ed", attended, dz_one_low, preferred_element_type=F32).astype(BF)
    g_out = jnp.pad(g_out.reshape(4, 8, 24, 768), ((0, 0), (0, 0), (0, 8), (0, 0))).reshape(4, 256, 768)
    d_att = jnp.einsum("ld,ed->le", dz_one_low, w_out, preferred_element_type=F32).astype(BF)
    d_att = d_att.reshape(512, 4, 3, HEAD_DIM)
    d_prob = jnp.einsum("qthe,tkhe->thqk", d_att, values, preferred_element_type=F32)
    d_values = jnp.einsum("thqk,qthe->tkhe", prob_low, d_att, preferred_element_type=F32)
    inner = jnp.sum(d_prob * attn_prob, axis=-1, keepdims=True)
    d_scores = (attn_prob * (d_prob - inner)).astype(BF)
    d_queries = jnp.einsum("thqk,tkhe->tqhe", d_scores, keys, preferred_element_type=F32) * scaling
    d_keys = jnp.einsum("thqk,tqhe->tkhe", d_scores, queries, preferred_element_type=F32) * scaling
    d_bias_q = jnp.sum(d_queries, axis=1).reshape(4, 192)
    d_bias_v = jnp.sum(d_values, axis=1).reshape(4, 192)
    d_qkv = jnp.stack([d_queries, d_keys, d_values], axis=2).astype(BF).reshape(4, 512, 576)
    g_qkv = jnp.einsum("ld,tle->tde", x_row, d_qkv, preferred_element_type=F32).astype(BF)
    input_grad = dz_one + jnp.einsum("tle,tde->ld", d_qkv, w_qkv, preferred_element_type=F32)

    shared = jnp.stack([d_bias_out, d_bias_down, d_gain_one, d_shift_one, d_gain_two, d_shift_two])
    shared = shared.reshape(6, 4, 192).transpose(1, 0, 2).reshape(4, 1152)
    small_grads = jnp.concatenate([d_bias_q, d_bias_v, d_bias_up, shared], axis=1)
    small_grads = jnp.pad(small_grads.reshape(4, 1, 18, 128), ((0, 0), (0, 0), (0, 6), (0, 0)))
    blocks, small_sum, out_mine, dx_mine, pool_all = reduce_call(
        g_qkv,
        g_out,
        g_up,
        g_down,
        small_grads,
        out_row,
        input_grad.astype(BF),
        pool_mean,
    )
    small_row = small_sum[:18].reshape(block_len)
    norm_grads = small_row[1152:].reshape(6, 192)
    pooled = lax.dynamic_slice_in_dim(pool_all, tensor_at * 192, 192, 2)

    wanted = data_at * per_owner + jnp.arange(per_owner, dtype=jnp.int32)
    block_of, filled = slot_blocks(slot_of, wanted)
    pick = (slot_order[None, :] == wanted[:, None]).astype(BF)
    owned = dot_f32(pick, blocks)
    owned = jnp.where((wanted == slot_of[768])[:, None], small_row[None], owned)
    token_position = block_of[:, None] * block_len + jnp.arange(block_len, dtype=jnp.int32)[None, :]
    step_rate, decay_on = step_rates(token_position, MODEL_WIDTH, FF, 4)
    new_master, new_first, new_second = adamw(
        owned,
        first_moment[0],
        second_moment[0],
        master_state[0],
        step_rate,
        decay_on,
        filled[:, None],
    )
    return (
        jnp.transpose(out_mine, (1, 0, 2)).astype(F32),
        pooled,
        jnp.transpose(dx_mine, (1, 0, 2)).astype(F32),
        new_master[None],
        new_first[None],
        new_second[None],
        norm_grads,
    )


def solution(mesh):
    in_specs = (
        P("tensor", "dp", None),
        P("dp", None),
        P("dp", None),
        P("tensor", "dp", None),
        P(),
        P("tensor", "dp", None),
        P("tensor", "dp", None),
        P("tensor", "dp", None),
    )
    out_specs = (
        P("tensor", "dp", None),
        P("dp", None, "tensor"),
        P("tensor", "dp", None),
        P("tensor", "dp", None),
        P("tensor", "dp", None),
        P("tensor", "dp", None),
        P(None, "tensor"),
    )
    plain = mesh.shape["dp"] != 8 or mesh.shape["tensor"] != 4
    body = local_general if plain else local_rows
    return jax.shard_map(body, mesh=mesh, in_specs=in_specs, out_specs=out_specs, check_vma=False)
```

profile of v0, /device:TPU:9, one launch (start us, length us, event | category | flops | bytes accessed | tf_op | source)
XLA Modules:
  0.0 362.2 jit_solution(16118634118147661869)
XLA Ops:
  0.7 0.8 compare_bitcast_fusion
  1.4 1.1 convert_reduce_fusion
  2.6 0.7 multiply_add_fusion
  3.3 0.5 slice.54
  3.8 1.2 broadcast_compare_fusion
  5.0 0.2 compare_reduce_fusion
  5.3 0.2 fusion.31
  5.7 0.1 reshape.176
  5.8 0.1 reshape.177
  5.8 1.2 broadcast_in_dim.100.small_slot
  7.4 1.3 fusion.39
  8.7 0.2 copy.78
  8.9 0.8 broadcast_in_dim.115.slot_col
  9.7 0.1 copy.79
  9.9 0.8 subtract_select_fusion.id_col
  10.6 2.5 copy_bitcast_fusion
  13.1 125.6 %gather_and_forward.1 = (bf16[4,768,576]{2,1,0:T(8,128)(2,1)}, bf16[4,256,768]{2,1,0:T(8,128)(2,1)}, bf16[4,768,768]{2,1,0:T(8,128)(2,1)}, bf16[4,768,768]{2,1,0...) custom-call(f32[192,2304]{1,0:T(8,128)} %bitcast.148, ...), custom_call_target="tpu_custom_call" | custom-call | tf_op jit(solution)/shard_map/gather_and_forward/pallas_call | solution.py:888
  138.7 4.5 %copy.83 = bf16[4,512,576]{1,2,0:T(8,128)(2,1)} copy(bf16[4,512,576]{2,1,0:T(8,128)(2,1)} %get-tuple-element.30) | data formatting | bytes 4718592 | tf_op jit(solution)/shard_map/gather_and_forward/pallas_call | solution.py:888
  143.2 0.2 slice_reduce_fusion.1
  143.4 1.0 slice_reduce_fusion.2
  144.4 0.1 reshape_squeeze.3
  144.7 0.7 multiply_reduce_fusion
  145.5 1.6 fusion.42
  147.3 1.4 copy.93
  148.7 7.3 %convolution_convert_fusion.g_down = bf16[4,768,768]{2,1,0:T(8,128)(2,1)} fusion(bf16[4,512,768]{2,1,0:T(8,128)(2,1)} %get-tuple-element.44, f32[512,768]{1,0:T(8,128)} %get-tuple-element.94), kind=kOutput, calls=%fused_computation.9 | convolution fusion | flops 2418671616 | bytes 9437184 | tf_op jit(solution)/shard_map/tlf,ld->tfd/dot_general | solution.py:1194
  156.0 4.7 %fusion.2 = (f32[4,768]{1,0:T(4,128)S(1)}, f32[4,768,512]{1,2,0:T(8,128)S(1)}) fusion(bf16[4,512,768]{2,1,0:T(8,128)(2,1)S(1)} %copy-done.2, bf16[4,768,768]{2,1,0:T(8,128)(2,1)} %get-tuple-element.36, f32[512,768]{1,0:T(8,128)S(1)} %copy-done.9), kind=kOutput, calls=%fused_computation.6 | convolution fusion | flops 2421027840 | bytes 15740928 | tf_op jit(solution)/shard_map/ld,tfd->tlf/dot_general | solution.py:1195
  160.8 8.8 %multiply_reduce_fusion.1 = (f32[768]{0:T(1024)S(1)}, f32[512]{0:T(512)S(1)}, f32[512]{0:T(512)S(1)}, f32[768]{0:T(1024)S(1)}, f32[512,768]{1,0:T(8,128)}) fusion(f32[512,768]{1,0:T(8,128)S(1)} %copy-done.13, f32[768]{0:T(1024)S(1)} %mul.183, f32[512,768]{1,0:T(8,128)S(1)} %copy-done.9, bf16[4,768,768]{2,1,0:T(8,128)(2,1)} %get-tuple-element.38, ...), kind=kOutput, calls=%fused_computation.44 | convolution fusion | flops 2423780864 | bytes 18887680 | tf_op jit(solution)/shard_map/tlf,tdf->ld/dot_general | solution.py:1200
  169.7 2.4 fusion.43
  172.1 1.7 convolution_convert_fusion.3
  173.9 2.3 copy.86
  176.3 0.1 reshape.188
  176.4 2.6 convolution_convert_fusion.2
  179.0 1.3 pad.8
  180.3 6.1 %convert_bitcast_fusion.g_up = bf16[4,768,768]{2,1,0:T(8,128)(2,1)} fusion(bf16[512,768]{1,0:T(8,128)(2,1)} %get-tuple-element.43, bf16[4,512,768]{2,1,0:T(8,128)(2,1)S(1)} %copy-done.2, f32[4,768,512]{1,2,0:T(8,128)S(1)} %copy-done.1), kind=kOutput, calls=%fused_computation.5 | convolution fusion | flops 2422996992 | bytes 14942208 | tf_op jit(solution)/shard_map/ld,tlf->tdf/dot_general | solution.py:1199
  186.4 1.9 bitcast_reduce_fusion
  188.3 9.2 %copy.85 = bf16[4,3,512,512]{2,3,1,0:T(8,128)(2,1)} copy(bf16[4,3,512,512]{3,2,1,0:T(8,128)(2,1)} %bitcast.133) | data formatting | bytes 12582912 | tf_op jit(solution)/shard_map/reshape | solution.py:1182
  197.6 0.1 reshape.187
  197.7 2.2 fusion.24
  199.9 4.8 %fusion = (f32[4,3,512]{2,1,0:T(4,128)S(1)}, f32[4,3,512,512]{2,3,1,0:T(8,128)S(1)}) fusion(bf16[4,3,512,512]{2,3,1,0:T(8,128)(2,1)} %copy.85, bf16[512,4,3,64]{0,3,2,1:T(8,128)(2,1)S(1)} %bitcast.142, bf16[4,512,3,3,64]{1,4,3,2,0:T(8,128)(2,1)S(1)} %bitcast.138), kind=kOutput, calls=%fused_computation.2 | convolution fusion | flops 412084224 | bytes 20471808 | tf_op jit(solution)/shard_map/qthe,tkhe->thqk/dot_general | solution.py:1210
  204.7 2.3 fusion.1
  207.1 2.0 fusion.22
  209.1 2.0 bitcast_reduce_fusion.1
  211.1 0.1 reshape.186
  211.1 0.1 concatenate.8
  211.3 0.6 pad.9.small_in
  211.9 1.2 fusion.23
  213.1 0.3 pad_maximum_fusion
  213.4 0.2 copy.91
  213.6 1.7 copy-done.18
  215.2 0.5 copy-done.7
  215.8 3.2 fusion.18.dx_row
  218.9 2.0 convolution_convert_fusion.1
  220.9 4.0 %copy.92 = bf16[4,576,768]{1,2,0:T(8,128)(2,1)} copy(bf16[4,576,768]{2,1,0:T(8,128)(2,1)S(1)} %convolution_convert_fusion.1) | data formatting | bytes 7077888 | tf_op jit(solution)/shard_map/convert_element_type | solution.py:1219
  224.9 121.5 %reduce_gradients.1 = (bf16[768,2304]{1,0:T(8,128)(2,1)}, f32[24,128]{1,0:T(8,128)}, bf16[4,128,768]{2,1,0:T(8,128)(2,1)}, bf16[4,128,768]{2,1,0:T(8,128)(2,1)}, f32[4,8,768]{2,1,0:T(8,128)}) custom-call(bf16[4,768,576]{2,1,0:T(8,128)(2,1)} %bitcast.137, bf16[4,256,768]{2,1,0:T(8,128)(2,1)} %bitcast.143, bf16[4,768,768]{2,1,0:T(8,128)(2,1)} %convert_bitcast_fusion.g_up, ...), custom_call_target="tpu_custom_call" | custom-call | tf_op jit(solution)/shard_map/reduce_gradients/pallas_call | solution.py:1084
  346.4 0.7 slice.64
  347.1 0.7 slice_bitcast_fusion.6
  347.8 0.7 reshape.190
  348.5 1.5 constant_dynamic-slice_fusion
  350.0 1.4 convert_bitcast_fusion.2
  351.4 2.2 copy.99
  353.6 0.1 convert_bitcast_fusion.1
  353.7 2.2 copy.100
  355.9 0.8 copy-done.12
  356.7 5.3 %select_bitcast_fusion = (f32[1,192,2304]{2,1,0:T(8,128)}, f32[1,192,2304]{2,1,0:T(8,128)}, f32[1,192,2304]{2,1,0:T(8,128)}) fusion(pred[192]{0:T(512)(128)(4,1)S(1)} %compare_reduce_fusion, f32[1,192,2304]{2,1,0:T(8,128)S(1)} %copy-done.20, f32[1,192,2304]{2,1,0:T(8,128)S(1)} %copy-done.21, s32[192]{0:T(256)S(1)} %broadcast_multiply_fusion.4, ...), kind=kOutput, calls=%fused_computation.18 | convolution fusion | flops 696434688 | bytes 14169984 | tf_op jit(solution)/shard_map/dot_general | solution.py:451
  (82 shorter events, 1.3 us)
Async XLA Ops:
  0.6 10.0 %copy-start.15 = (bf16[128,4,768]{2,1,0:T(4,128)(2,1)S(1)}, bf16[128,4,768]{2,1,0:T(4,128)(2,1)}, u32[]{:S(2)}) copy-start(bf16[128,4,768]{2,1,0:T(4,128)(2,1)} %param.11) | copy-start | bytes 2359300
  138.7 4.5 %copy-start.17 = (f32[2,512,1]{2,1,0:T(8,128)S(1)}, f32[2,512,1]{2,1,0:T(8,128)}, u32[]{:S(2)}) copy-start(f32[2,512,1]{2,1,0:T(8,128)} %get-tuple-element.32) | copy-start | bytes 12292
  138.7 6.0 %copy-start.8 = (f32[512,768]{1,0:T(8,128)S(1)}, f32[512,768]{1,0:T(8,128)}, u32[]{:S(2)}) copy-start(f32[512,768]{1,0:T(8,128)} %get-tuple-element.35) | copy-start | bytes 4718596
  138.7 6.0 %copy-start.11 = (bf16[512,768]{1,0:T(8,128)(2,1)S(1)}, bf16[512,768]{1,0:T(8,128)(2,1)}, u32[]{:S(2)}) copy-start(bf16[512,768]{1,0:T(8,128)(2,1)} %get-tuple-element.33) | copy-start | bytes 2359300
  145.5 1.8 copy-start.14
  148.7 7.3 %copy-start.2 = (bf16[4,512,768]{2,1,0:T(8,128)(2,1)S(1)}, bf16[4,512,768]{2,1,0:T(8,128)(2,1)}, u32[]{:S(2)}) copy-start(bf16[4,512,768]{2,1,0:T(8,128)(2,1)} %get-tuple-element.37) | copy-start | bytes 9437188
  148.7 7.3 %copy-start.9 = (f32[512,768]{1,0:T(8,128)S(1)}, f32[512,768]{1,0:T(8,128)}, u32[]{:S(2)}) copy-start(f32[512,768]{1,0:T(8,128)} %get-tuple-element.94) | copy-start | bytes 4718596
  156.0 4.7 %copy-start.13 = (f32[512,768]{1,0:T(8,128)S(1)}, f32[512,768]{1,0:T(8,128)}, u32[]{:S(2)}) copy-start(f32[512,768]{1,0:T(8,128)} %get-tuple-element.39) | copy-start | bytes 4718596
  160.7 8.9 %copy-start = (f32[4,768,512]{1,2,0:T(8,128)}, f32[4,768,512]{1,2,0:T(8,128)S(1)}, u32[]{:S(2)}) copy-start(f32[4,768,512]{1,2,0:T(8,128)S(1)} %get-tuple-element.113) | copy-start | bytes 18874372
  169.7 2.4 copy-start.22
  172.1 1.7 copy-start.6
  176.4 3.9 %copy-start.1 = (f32[4,768,512]{1,2,0:T(8,128)S(1)}, f32[4,768,512]{1,2,0:T(8,128)}, u32[]{:S(2)}) copy-start(f32[4,768,512]{1,2,0:T(8,128)} %copy-done) | copy-start | bytes 18874372
  179.0 7.4 %slice-start.2 = ((s8[6291456]{0:T(1024)(128)(4,1)}), s8[4194304]{0:T(1024)(128)(4,1)S(1)}, s32[]{:S(2)}) async-start(s8[6291456]{0:T(1024)(128)(4,1)} %bitcast.134), calls=%async_computation.2 | async-start | bytes 8388608
  180.3 6.1 %slice-start.3 = ((s8[6291456]{0:T(1024)(128)(4,1)}), s8[2097152]{0:T(1024)(128)(4,1)S(1)}, s32[]{:S(2)}) async-start(s8[6291456]{0:T(1024)(128)(4,1)} %bitcast.134), calls=%async_computation.3 | async-start | bytes 4194304
  180.3 6.1 %copy-start.4 = (bf16[512,768]{0,1:T(8,128)(2,1)S(1)}, bf16[512,768]{0,1:T(8,128)(2,1)}, u32[]{:S(2)}) copy-start(bf16[512,768]{0,1:T(8,128)(2,1)} %copy.86) | copy-start | bytes 2359300
  188.3 11.5 %copy-start.3 = (bf16[4,512,576]{1,2,0:T(8,128)(2,1)S(1)}, bf16[4,512,576]{1,2,0:T(8,128)(2,1)}, u32[]{:S(2)}) copy-start(bf16[4,512,576]{1,2,0:T(8,128)(2,1)} %copy.83) | copy-start | bytes 7077892
  197.6 2.3 copy-start.5
  197.7 7.0 %slice-start = ((s8[6291456]{0:T(1024)(128)(4,1)}), s8[4194304]{0:T(1024)(128)(4,1)S(1)}, s32[]{:S(2)}) async-start(s8[6291456]{0:T(1024)(128)(4,1)} %bitcast.131), calls=%async_computation | async-start | bytes 8388608
  199.9 4.8 %slice-start.1 = ((s8[6291456]{0:T(1024)(128)(4,1)}), s8[2097152]{0:T(1024)(128)(4,1)S(1)}, s32[]{:S(2)}) async-start(s8[6291456]{0:T(1024)(128)(4,1)} %bitcast.131), calls=%async_computation.1 | async-start | bytes 4194304
  211.1 2.0 copy-start.10
  213.1 2.1 copy-start.18
  213.4 2.4 copy-start.7
  215.8 3.2 copy-start.23
  350.0 5.9 %copy-start.21 = (f32[1,192,2304]{2,1,0:T(8,128)S(1)}, f32[1,192,2304]{2,1,0:T(8,128)}, u32[]{:S(2)}) copy-start(f32[1,192,2304]{2,1,0:T(8,128)} %param.14) | copy-start | bytes 5308420
  351.4 2.2 copy-start.16
  351.4 4.5 %copy-start.20 = (f32[1,192,2304]{2,1,0:T(8,128)S(1)}, f32[1,192,2304]{2,1,0:T(8,128)}, u32[]{:S(2)}) copy-start(f32[1,192,2304]{2,1,0:T(8,128)} %param.15) | copy-start | bytes 5308420
  353.6 2.3 copy-start.19
  353.7 3.0 copy-start.12
  353.7 3.0 copy-start.24
where the time goes:
time: 366 us; the launch traced here: 362 us
  Pallas kernels  247 us (67%)
  matrix products  52.3 us (14%)
  local copies, waits for them, and re-layouts  46.3 us (13%)
  other arithmetic  15.3 us (4%)
    pallas_call x1, Pallas kernels, forward_call(): pl.pallas_call(forward_kernel, out_shape=[shape(*o) for o in outs], in_sp...  126 us
    pallas_call x1, Pallas kernels, reduce_call(): pl.pallas_call(reduce_kernel, out_shape=[shape((768, 2304), BF), shape((2...  122 us
    reshape x1, local copies, waits for them, and re-layouts, local_rows(): prob_low = prob_low.reshape(4, 3, 512, 512)  9.22 us
    dot_general x1, matrix products, local_rows(): jnp.einsum('tlf,tdf->ld', d_up_low, w_up, preferred_element_type=F32)  8.83 us
    unnamed x60, local copies, waits for them, and re-layouts  7.47 us

commit v1 on v0

--- a/solution.py
+++ b/solution.py
@@ -414,6 +414,10 @@
         copy = pltpu.make_async_copy(src, dst, self.sems[2].at[i])
         copy.start()
         return copy
+
+    def sent(self, copy):
+        copy.wait_send()
+        self.open = [other for other in self.open if other is not copy]
 
     def finish(self):
         for copy in self.open:
@@ -903,25 +907,26 @@
     )(master, slot_col, small_slot, id_col, id_row, x_in, gy_in)
 
 
-def add_into(total, other, rows, step):
-    groups = other.shape[0]
-
-    @pl.loop(0, groups * (rows // step))
-    def _(i):
-        g = i // (rows // step)
-        at = pl.ds(pl.multiple_of((i % (rows // step)) * step, step), step)
-        total[g, at, :] = total[g, at, :] + other[g, at, :]
-
-
-def reduce_kernel(
-    g_qkv,
-    g_out,
-    g_up,
-    g_down,
+def backward_kernel(
+    flag_col,
+    out_row,
+    pool_in,
+    gy_in,
+    n_two_in,
+    inv_in,
     small_in,
-    out_row,
-    dx_row,
-    pool_in,
+    act_in,
+    pull_in,
+    w_down,
+    w_up,
+    h_in,
+    n_one_in,
+    att_in,
+    w_out,
+    qkv_in,
+    prob_in,
+    w_qkv,
+    x_in,
     blocks,
     small_out,
     out_mine,
@@ -930,189 +935,511 @@
     *scratch,
 ):
     sums, cores, lefts, tops, lefts_two, tops_two, deeps = (scratch[4 * i : 4 * i + 4] for i in range(7))
-    share, share_low, small_sum, small_land, send_sems, recv_sems, local_sems = scratch[28:]
+    (
+        ring,
+        ring_narrow,
+        share,
+        share_low,
+        small_grad,
+        small_land,
+        small,
+        norm,
+        gy,
+        normed,
+        inv,
+        act,
+        pull,
+        v_down,
+        v_up,
+        h_low,
+        att,
+        v_out,
+        qkv,
+        prob,
+        v_qkv,
+        x_row,
+        wide,
+        low,
+        total,
+        d_up,
+        d_att,
+        d_qkv,
+        turned,
+        go,
+        reds,
+        red_up,
+        red_qv,
+        send_sems,
+        recv_sems,
+        local_sems,
+    ) = scratch[28:]
     place = Place()
     link = Sender(send_sems, recv_sems, local_sems)
-    grads = (g_qkv, g_out, g_up, g_down)
-    loads = {}
-    order = (3, 2, 1, 0)
-    for w in order:
-        rows = WEIGHTS[w][1]
-        loads[w] = link.copy(grads[w].at[:, half_of(place, rows)], sums[w])
+    t_of = place.ahead
+    steps = (1, 2, 3, 0)
+    got = {}
+
+    def load(name, src, dst):
+        got[name] = link.copy(src, dst)
+
+    load("small", small_in, small)
+    load("normed", n_two_in, normed)
+    load("gy", gy_in, gy)
+    load("inv", inv_in, inv)
+
+    def load_ffn(i):
+        t, slot = t_of[steps[i]], i % 2
+        load(("act", i), act_in.at[t], act.at[slot])
+        load(("down", i), w_down.at[t], v_down.at[slot])
+        load(("pull", i), pull_in.at[t], pull.at[slot])
+        load(("up", i), w_up.at[t], v_up.at[slot])
+
+    def load_att(i):
+        t, slot = t_of[steps[i]], i % 2
+        load(("prob", i), prob_in.at[pl.ds(3 * t, 3)], prob.at[slot])
+        load(("qkv", i), w_qkv.at[t], v_qkv.at[slot])
+
+    load_ffn(0)
+    load("h", h_in, h_low)
+    load_ffn(1)
+    load("att", att_in, att)
+    load("wout", w_out, v_out)
+    load("qkvs", qkv_in, qkv)
+    load("x", x_in, x_row)
+    load_att(0)
+    load_att(1)
     place.greet()
-    t, x, y = place.t, place.x, place.y
-    core_moves = {}
-    for w in order:
-        rows = WEIGHTS[w][1]
-        other = pl.ds(pl.multiple_of((1 - place.c) * (4 * rows), 128), 4 * rows)
-        core_moves[w] = link.send(grads[w].at[:, other], cores[w], place.core)
-    moves = []
-    stay = [link.copy(small_in.at[t], small_sum.at[pl.ds(0, 1)])]
-    small_moves = [link.send(small_in.at[place.ahead[k]], small_land.at[k - 1], place.deep[k]) for k in (1, 2, 3)]
-    for src, dst in ((out_row, out_mine), (dx_row, dx_mine)):
-        stay.append(link.copy(src.at[pl.ds(pl.multiple_of(t * 128, 128), 128)], dst.at[t]))
-        for k in (1, 2, 3):
-            part = src.at[pl.ds(pl.multiple_of(place.ahead[k] * 128, 128), 128)]
-            moves.append(link.send(part, dst.at[t], place.deep[k]))
+    t, x, y, c = place.t, place.x, place.y, place.c
+
+    moves, stay = [], []
+    stay.append(link.copy(out_row.at[pl.ds(pl.multiple_of(t * 128, 128), 128)], out_mine.at[t]))
     stay.append(link.copy(pool_in, pool_out.at[t]))
     for k in (1, 2, 3):
+        part = out_row.at[pl.ds(pl.multiple_of(t_of[k] * 128, 128), 128)]
+        moves.append(link.send(part, out_mine.at[t], place.deep[k]))
         moves.append(link.send(pool_in, pool_out.at[t], place.deep[k]))
 
-    first, second, third = {}, {}, {}
-
-    def chip_row(w, yy, xx, half):
+    core_moves, first, second, third = {}, {}, {}, {}
+    ring_open = [None] * 5
+    ring_at = [0, 0]
+
+    def chip_row(w, k, yy, xx, half):
         rows = WEIGHTS[w][1]
         at = pl.multiple_of((yy * 2 + xx) * rows + half * (rows // 2), 16)
-        return sums[w].at[:, pl.ds(at, rows // 2)]
-
-    def add(total, other):
-        groups, rows, _ = other.shape
-        add_into(total, other, rows, 16)
-
-    def stage_core(w):
-        loads[w].wait()
-        core_moves[w].wait_recv()
-        add_into(sums[w], cores[w], 4 * WEIGHTS[w][1], 32)
-        first[w] = []
+        return sums[w].at[t_of[k], pl.ds(at, rows // 2)]
+
+    def produce(w, k, make):
+        narrow = w == 0
+        slot = 3 + ring_at[1] % 2 if narrow else ring_at[0] % 3
+        ring_at[narrow] += 1
+        if ring_open[slot] is not None:
+            link.sent(ring_open[slot])
+        cols, rows = WEIGHTS[w]
+        away = ring_narrow.at[slot - 3] if narrow else ring.at[slot, pl.ds(0, 4 * rows)]
+        away[...] = make(1 - c).astype(BF)
+        move = link.send(away, cores[w].at[k], place.core)
+        ring_open[slot] = move
+        core_moves[w, k] = move
+        sums[w][t_of[k]] = make(c).astype(BF)
+
+    def core_add(w, k):
+        core_moves[w, k].wait_recv()
+        rows = WEIGHTS[w][1]
+
+        @pl.loop(0, 4)
+        def _(i):
+            at = pl.ds(pl.multiple_of(i * rows, 32), rows)
+            sums[w][t_of[k], at, :] += cores[w][k, at, :]
+
+        first[w, k] = []
         for i in (0, 1):
-            first[w].append(link.send(chip_row(w, i, 1 - x, 0), lefts[w].at[i], place.right))
-            first[w].append(link.send(chip_row(w, 1 - y, i, 1), tops[w].at[i], place.down))
-
-    def stage_plane(w):
-        for move in first[w]:
+            first[w, k].append(link.send(chip_row(w, k, i, 1 - x, 0), lefts[w].at[k, i], place.right))
+            first[w, k].append(link.send(chip_row(w, k, 1 - y, i, 1), tops[w].at[k, i], place.down))
+
+    def add(spot, other):
+        spot[...] = spot[...] + other[...]
+
+    def plane_add(w, k):
+        for move in first[w, k]:
             move.wait_recv()
-        add(chip_row(w, 1 - y, x, 0), lefts[w].at[1 - y])
-        add(chip_row(w, y, 1 - x, 1), tops[w].at[1 - x])
-        second[w] = [
-            link.send(chip_row(w, 1 - y, x, 0), lefts_two[w], place.down),
-            link.send(chip_row(w, y, 1 - x, 1), tops_two[w], place.right),
+        down_part, right_part = chip_row(w, k, 1 - y, x, 0), chip_row(w, k, y, 1 - x, 1)
+        add(down_part, lefts[w].at[k, 1 - y])
+        add(right_part, tops[w].at[k, 1 - x])
+        second[w, k] = [
+            link.send(down_part, lefts_two[w].at[k], place.down),
+            link.send(right_part, tops_two[w].at[k], place.right),
         ]
-        add(chip_row(w, y, x, 0), lefts[w].at[y])
-        add(chip_row(w, y, x, 1), tops[w].at[x])
-
-    def stage_deep(w):
-        for move in second[w]:
+        add(chip_row(w, k, y, x, 0), lefts[w].at[k, y])
+        add(chip_row(w, k, y, x, 1), tops[w].at[k, x])
+
+    def deep_add(w, k):
+        for move in second[w, k]:
             move.wait_recv()
-        add(chip_row(w, y, x, 0), lefts_two[w])
-        add(chip_row(w, y, x, 1), tops_two[w])
+        add(chip_row(w, k, y, x, 0), lefts_two[w].at[k])
+        add(chip_row(w, k, y, x, 1), tops_two[w].at[k])
+        rows = WEIGHTS[w][1]
+        if k:
+            spot = pl.ds(pl.multiple_of(place.xy * rows, 16), rows)
+            third[w, k] = link.send(sums[w].at[t_of[k], spot], deeps[w].at[k - 1], place.deep[k])
+
+    def end(w):
         rows = WEIGHTS[w][1]
         spot = pl.ds(pl.multiple_of(place.xy * rows, 16), rows)
-        third[w] = [
-            link.send(sums[w].at[place.ahead[k], spot], deeps[w].at[k - 1], place.deep[k])
-            for k in (1, 2, 3)
-        ]
-
-    def stage_end(w):
-        for move in third[w]:
-            move.wait_recv()
-        rows = WEIGHTS[w][1]
-        spot = pl.ds(pl.multiple_of(place.xy * rows, 16), rows)
-        total = sums[w][t, spot, :].astype(F32)
-        for k in range(3):
-            total = total + deeps[w][k].astype(F32)
-        total = total.astype(BF)
-        turned = (((0,), (0,)), ((), ()))
+        whole = sums[w][t, spot, :].astype(F32)
+        for k in (1, 2, 3):
+            third[w, k].wait_recv()
+            whole = whole + deeps[w][k - 1].astype(F32)
+        whole = whole.astype(BF)
         if w == 0:
-            parts = lax.dot_general(interleave(96, 4), total, turned, preferred_element_type=F32)
+            parts = dot_tn(interleave(96, 4), whole)
             share[64:88, :] = jnp.concatenate([parts[24 * r : 24 * r + 24] for r in range(4)], axis=1)
         elif w == 1:
-            parts = lax.dot_general(interleave_out(), total, turned, preferred_element_type=F32)
+            parts = dot_tn(interleave_out(), whole)
             for k in range(3):
                 share[88:96, 768 * k : 768 * k + 768] = parts[8 * k : 8 * k + 8]
         else:
             at = 0 if w == 2 else 32
-            parts = lax.dot_general(interleave(96, 3), total, turned, preferred_element_type=F32)
+            parts = dot_tn(interleave(96, 3), whole)
             for k in range(3):
                 share[at : at + 32, 768 * k : 768 * k + 768] = parts[32 * k : 32 * k + 32]
 
-    stage_core(3)
-    stage_core(2)
-    stage_plane(3)
-    stage_core(1)
-    stage_core(0)
-    stage_deep(3)
-    stage_plane(2)
-    stage_plane(1)
-    stage_deep(2)
-    stage_plane(0)
-    stage_end(3)
-    stage_deep(1)
-
-    stay[0].wait()
+    def column_sum(value):
+        return jnp.sum(value, axis=0, keepdims=True)
+
+    def norm_two_back():
+        def body(rows):
+            grad = gy[rows, :].astype(F32) * flag_col[rows, :]
+            n = normed[rows, :]
+            dz = norm_back(grad * norm[4:5, :], n, inv[1, rows, :])
+            wide[rows, :] = dz
+            total[rows, :] = dz
+            low[rows, :] = dz.astype(BF)
+            reds[4:5, :] += column_sum(grad * n)
+            reds[5:6, :] += column_sum(grad)
+            reds[1:2, :] += column_sum(dz)
+
+        row_loop(body)
+
+    def lanes(which):
+        return pl.ds(pl.multiple_of(which * 384, 128), 384)
+
+    def down_piece(i):
+        k, slot = steps[i], i % 2
+        got["act", i].wait()
+        produce(3, k, lambda which: dot_tn(act[slot, :, lanes(which)], low[...]))
+
+    def up_piece(i):
+        k, slot = steps[i], i % 2
+        got["down", i].wait()
+        got["pull", i].wait()
+
+        def body(rows):
+            grad = dot_nt(low[rows, :], v_down[slot]) * pull[slot, rows, :].astype(F32)
+            red_up[t_of[k]] += column_sum(grad)
+            d_up[rows, :] = grad.astype(BF)
+
+        row_loop(body, 256)
+        if i == 0:
+            got["h"].wait()
+        produce(2, k, lambda which: dot_tn(h_low[:, lanes(which)], d_up[...]))
+
+    def hidden_back(i):
+        slot = i % 2
+        got["up", i].wait()
+
+        def body(rows):
+            total[rows, :] += dot_nt(d_up[rows, :], v_up[slot])
+
+        row_loop(body, 256)
+        if i + 2 < 4:
+            load_ffn(i + 2)
+        if i == 1:
+            load("n_one", n_one_in, normed)
+
+    def norm_one_back():
+        got["n_one"].wait()
+
+        def body(rows):
+            dh = total[rows, :]
+            n = normed[rows, :]
+            dz = norm_back(dh * norm[2:3, :], n, inv[0, rows, :])
+            total[rows, :] = dz
+            low[rows, :] = dz.astype(BF)
+            reds[2:3, :] += column_sum(dh * n)
+            reds[3:4, :] += column_sum(dh)
+            reds[0:1, :] += column_sum(dz)
+
+        row_loop(body)
+
+    def out_piece(i):
+        k = steps[i]
+        if i == 0:
+            got["att"].wait()
+            got["wout"].wait()
+        go[...] = dot_tn(att[t_of[k]], low[...])
+
+        def make(which):
+            part = go[pl.ds(pl.multiple_of(which * 96, 96), 96), :]
+            pad = jnp.zeros((8, 768), F32)
+            parts = []
+            for j in range(4):
+                parts += [part[24 * j : 24 * j + 24], pad]
+            return jnp.concatenate(parts, axis=0)
+
+        produce(1, k, make)
+
+        def body(rows):
+            d_att[rows, :] = dot_nt(low[rows, :], v_out[t_of[k]]).astype(BF)
+
+        row_loop(body, 256)
+
+    def attention_back(i):
+        k, slot = steps[i], i % 2
+        tk = t_of[k]
+        if i == 0:
+            got["qkvs"].wait()
+        got["prob", i].wait()
+        turned[...] = jnp.zeros_like(turned)
+
+        def body(rows):
+            d_queries = []
+            for j in range(3):
+                at = 64 * j
+                grad = d_att[rows, at : at + 64]
+                weight_low = prob[slot, j, rows, :]
+                weight = weight_low.astype(F32)
+                d_prob = dot_nt(grad, qkv[tk, :, 384 + at : 448 + at]) * weight
+                inner = jnp.sum(d_prob, axis=1, keepdims=True)
+                d_scores = (d_prob - weight * inner).astype(BF)
+                d_queries.append(dot_f32(d_scores, qkv[tk, :, 192 + at : 256 + at]))
+                turned[at : at + 64, :] += dot_tn(qkv[tk, rows, at : at + 64], d_scores)
+                turned[192 + at : 256 + at, :] += dot_tn(grad, weight_low)
+            dq = jnp.concatenate(d_queries, axis=1) * 0.125
+            red_qv[tk, :, :192] += column_sum(dq)
+            d_qkv[rows, :192] = dq.astype(BF)
+
+        row_loop(body, 256)
+        dk = jnp.transpose(turned[:192, :]) * 0.125
+        dv = jnp.transpose(turned[192:, :])
+        red_qv[tk, :, 192:] += column_sum(dv)
+        d_qkv[:, 192:] = jnp.concatenate([dk, dv], axis=1).astype(BF)
+
+    def qkv_piece(i):
+        k, slot = steps[i], i % 2
+        if i == 0:
+            got["x"].wait()
+        produce(0, k, lambda which: dot_tn(x_row[:, lanes(which)], d_qkv[...]))
+        got["qkv", i].wait()
+
+        def body(rows):
+            total[rows, :] += dot_nt(d_qkv[rows, :], v_qkv[slot])
+
+        row_loop(body, 256)
+        if i + 2 < 4:
+            load_att(i + 2)
+
+    got["small"].wait()
+    norm_vectors(small, norm)
+    reds[...] = jnp.zeros_like(reds)
+    red_up[...] = jnp.zeros_like(red_up)
+    red_qv[...] = jnp.zeros_like(red_qv)
+    small_grad[...] = jnp.zeros_like(small_grad)
+    for name in ("normed", "gy", "inv"):
+        got[name].wait()
+    norm_two_back()
+    a, b, d, e = ((3, k) for k in steps)
+    f, g, h, j = ((2, k) for k in steps)
+    down_piece(0)
+    up_piece(0)
+    core_add(*a)
+    hidden_back(0)
+    core_add(*f)
+    down_piece(1)
+    plane_add(*a)
+    up_piece(1)
+    core_add(*b)
+    hidden_back(1)
+    core_add(*g)
+    plane_add(*f)
+    down_piece(2)
+    deep_add(*a)
+    core_add(*d)
+    up_piece(2)
+    plane_add(*b)
+    deep_add(*f)
+    hidden_back(2)
+    core_add(*h)
+    down_piece(3)
+    core_add(*e)
+    up_piece(3)
+    plane_add(*g)
+    deep_add(*b)
+    hidden_back(3)
+    core_add(*j)
+    norm_one_back()
+    plane_add(*d)
+    deep_add(*g)
+    out_piece(0)
+    attention_back(0)
+    plane_add(*h)
+    deep_add(*d)
+    core_add(1, 1)
+    qkv_piece(0)
+    plane_add(*e)
+    deep_add(*h)
+    core_add(0, 1)
+    out_piece(1)
+    attention_back(1)
+    core_add(1, 2)
+    qkv_piece(1)
+    plane_add(*j)
+    deep_add(*e)
+    core_add(0, 2)
+    out_piece(2)
+    attention_back(2)
+    core_add(1, 3)
+    deep_add(*j)
+    plane_add(1, 1)
+    qkv_piece(2)
+    core_add(0, 3)
+    plane_add(0, 1)
+    deep_add(1, 1)
+    out_piece(3)
+    attention_back(3)
+    core_add(1, 0)
+    qkv_piece(3)
+    core_add(0, 0)
+
+    def dx_body(rows):
+        low[rows, :] = total[rows, :].astype(BF)
+
+    row_loop(dx_body)
+    own_rows = pl.ds(pl.multiple_of(t * 128, 128), 128)
+    stay.append(link.copy(low.at[own_rows], dx_mine.at[t]))
+    for k in (1, 2, 3):
+        part = low.at[pl.ds(pl.multiple_of(t_of[k] * 128, 128), 128)]
+        moves.append(link.send(part, dx_mine.at[t], place.deep[k]))
+    for q in range(4):
+        at = slice(192 * q, 192 * q + 192)
+        small_grad[q, 0:1, :] = jnp.concatenate(
+            [red_qv[q], red_up[q]] + [reds[i : i + 1, at] for i in range(6)], axis=1
+        )
+    small_sum = small_land.at[6]
+    small_keep = link.copy(small_grad.at[t], small_sum)
+    small_moves = [link.send(small_grad.at[t_of[k]], small_land.at[k - 1], place.deep[k]) for k in (1, 2, 3)]
+    plane_add(1, 2)
+    deep_add(0, 1)
+    plane_add(0, 2)
+    deep_add(1, 2)
+    plane_add(1, 3)
+    deep_add(0, 2)
+    plane_add(0, 3)
+    deep_add(1, 3)
+    end(3)
+    end(2)
+    plane_add(1, 0)
+    plane_add(0, 0)
+    deep_add(0, 3)
+    deep_add(1, 0)
+    deep_add(0, 0)
+    end(1)
+    small_keep.wait()
     for move in small_moves:
         move.wait_recv()
-    small_sum[0] = (
-        small_sum[0] + small_land[0, 0] + small_land[1, 0] + small_land[2, 0]
-    )
-    stage_end(2)
-    stage_deep(0)
-    stage_end(1)
+    small_land[7] = small_land[6] + small_land[0] + small_land[1] + small_land[2]
     for i, peer in enumerate((place.core, place.right, place.down)):
-        move = link.send(
-            small_sum.at[pl.ds(i, 1)], small_land.at[3 + i], peer
-        )
+        move = link.send(small_land.at[7 + i], small_land.at[3 + i], peer)
+        if i == 1:
+            end(0)
+            share_low[...] = share[...].astype(BF)
+            dest = pl.ds(pl.multiple_of((c * 4 + place.xy) * 96, 96), 96)
+            kept = link.copy(share_low, blocks.at[dest])
+            last = [
+                link.send(share_low, blocks.at[dest], to)
+                for to in (place.diag, place.right, place.down)
+            ]
         move.wait_recv()
-        small_sum[i + 1] = small_sum[i] + small_land[3 + i, 0]
-    stage_end(0)
-    small_out[...] = small_sum[3]
-
-    share_low[...] = share[...].astype(BF)
-    dest = pl.ds(pl.multiple_of((place.c * 4 + place.xy) * 96, 96), 96)
-    keep = link.copy(share_low, blocks.at[dest])
-    last = [link.send(share_low, blocks.at[dest], peer) for peer in (place.diag, place.right, place.down)]
-    keep.wait()
+        small_land[8 + i] = small_land[7 + i] + small_land[3 + i]
+    small_out[...] = small_land[10]
+    kept.wait()
     for move in last:
         move.wait_recv()
-    half = pl.ds(pl.multiple_of(place.c * 384, 384), 384)
+    half = pl.ds(pl.multiple_of(c * 384, 384), 384)
     across = link.send(blocks.at[half], blocks.at[half], place.core)
     across.wait_recv()
     for move in moves:
         move.wait_recv()
-    for copy in stay[1:]:
+    for copy in stay:
         copy.wait()
     link.finish()
 
 
-def reduce_call(g_qkv, g_out, g_up, g_down, small_in, out_row, dx_row, pool_in):
+def backward_call(*args):
     anywhere = pl.BlockSpec(memory_space=pl.ANY)
     vmem = pl.BlockSpec(memory_space=pltpu.VMEM)
     shape = jax.ShapeDtypeStruct
-    sums = [pltpu.VMEM((4, 4 * rows, cols), BF) for cols, rows in WEIGHTS]
-    halves = [pltpu.VMEM((2, 4, rows // 2, cols), BF) for cols, rows in WEIGHTS]
-    singles = [pltpu.VMEM((4, rows // 2, cols), BF) for cols, rows in WEIGHTS]
-    deeps = [pltpu.VMEM((3, rows, cols), BF) for cols, rows in WEIGHTS]
+    sums = [((4, 4 * rows, cols), BF) for cols, rows in WEIGHTS]
+    halves = [((4, 2, rows // 2, cols), BF) for cols, rows in WEIGHTS]
+    singles = [((4, rows // 2, cols), BF) for cols, rows in WEIGHTS]
+    deeps = [((3, rows, cols), BF) for cols, rows in WEIGHTS]
+    rest = [
+        ((3, 384, 768), BF),
+        ((2, 384, 576), BF),
+        ((96, 2304), F32),
+        ((96, 2304), BF),
+        ((4, 8, 2304), F32),
+        ((11, 8, 2304), F32),
+        ((4, 8, 2304), F32),
+        ((8, 768), F32),
+        ((512, 768), BF),
+        ((512, 768), F32),
+        ((2, 512, 1), F32),
+        ((2, 512, 768), BF),
+        ((2, 512, 768), BF),
+        ((2, 768, 768), BF),
+        ((2, 768, 768), BF),
+        ((512, 768), BF),
+        ((4, 512, 192), BF),
+        ((4, 192, 768), BF),
+        ((4, 512, 576), BF),
+        ((2, 3, 512, 512), BF),
+        ((2, 768, 576), BF),
+        ((512, 768), BF),
+        ((512, 768), F32),
+        ((512, 768), BF),
+        ((512, 768), F32),
+        ((512, 768), BF),
+        ((512, 192), BF),
+        ((512, 576), BF),
+        ((384, 512), F32),
+        ((192, 768), F32),
+        ((8, 768), F32),
+        ((4, 1, 768), F32),
+        ((4, 1, 384), F32),
+    ]
+    scratch = sums + sums + halves + halves + singles + singles + deeps + rest
     return pl.pallas_call(
-        reduce_kernel,
+        backward_kernel,
         out_shape=[
             shape((768, 2304), BF),
-            shape((24, 128), F32),
+            shape((8, 2304), F32),
             shape((4, 128, 768), BF),
             shape((4, 128, 768), BF),
             shape((4, 8, 768), F32),
         ],
-        in_specs=[anywhere] * 8,
+        in_specs=[vmem] + [anywhere] * 18,
         out_specs=[anywhere, vmem, anywhere, anywhere, anywhere],
-        scratch_shapes=sums
-        + sums
-        + halves
-        + halves
-        + singles
-        + singles
-        + deeps
+        scratch_shapes=[pltpu.VMEM(*s) for s in scratch]
         + [
-            pltpu.VMEM((96, 2304), F32),
-            pltpu.VMEM((96, 2304), BF),
-            pltpu.VMEM((4, 24, 128), F32),
-            pltpu.VMEM((6, 1, 24, 128), F32),
-            pltpu.SemaphoreType.DMA((80,)),
-            pltpu.SemaphoreType.DMA((80,)),
-            pltpu.SemaphoreType.DMA((12,)),
+            pltpu.SemaphoreType.DMA((160,)),
+            pltpu.SemaphoreType.DMA((160,)),
+            pltpu.SemaphoreType.DMA((64,)),
         ],
         compiler_params=pltpu.CompilerParams(
-            collective_id=1, has_side_effects=True, vmem_limit_bytes=56 * MIB
+            collective_id=1, has_side_effects=True, vmem_limit_bytes=62 * MIB
         ),
-        name="reduce_gradients",
-    )(g_qkv, g_out, g_up, g_down, small_in, out_row, dx_row, pool_in)
+        name="backward_and_reduce",
+    )(*args)
 
 
 def local_rows(
@@ -1174,66 +1501,28 @@
         jnp.transpose(layer_input_rows, (1, 0, 2)),
         jnp.transpose(output_gradient, (1, 0, 2)),
     )
-    norm_all = small_all[:, 0, 1152:].reshape(4, 6, 192).transpose(1, 0, 2).reshape(6, 768)
-    gain_one, gain_two = norm_all[2], norm_all[4]
-    qkv = qkv.reshape(4, 512, 3, 3, HEAD_DIM)
-    queries, keys, values = (qkv[:, :, i] for i in range(3))
-    scaling = HEAD_DIM ** (-0.5)
-    prob_low = prob_low.reshape(4, 3, 512, 512)
-    attn_prob = prob_low.astype(F32)
-    inv_one, inv_two = inverse[0], inverse[1]
-    w_out = w_out.reshape(768, 768)
-    attended = attended.transpose(1, 0, 2).reshape(512, 768)
-
-    grad_out = gy_row.astype(F32) * flags[:, None].astype(F32)
-    d_gain_two = jnp.sum(grad_out * normed_two, axis=0)
-    d_shift_two = jnp.sum(grad_out, axis=0)
-    dz_two = norm_back(grad_out * gain_two, normed_two, inv_two)
-    d_bias_down = jnp.sum(dz_two, axis=0)
-    dz_two_low = dz_two.astype(BF)
-    g_down = jnp.einsum("tlf,ld->tfd", act, dz_two_low, preferred_element_type=F32).astype(BF)
-    d_act = jnp.einsum("ld,tfd->tlf", dz_two_low, w_down, preferred_element_type=F32)
-    d_up = d_act * pull.astype(F32)
-    d_bias_up = jnp.sum(d_up, axis=1)
-    d_up_low = d_up.astype(BF)
-    g_up = jnp.einsum("ld,tlf->tdf", h_low, d_up_low, preferred_element_type=F32).astype(BF)
-    dh = dz_two + jnp.einsum("tlf,tdf->ld", d_up_low, w_up, preferred_element_type=F32)
-    d_gain_one = jnp.sum(dh * normed_one, axis=0)
-    d_shift_one = jnp.sum(dh, axis=0)
-    dz_one = norm_back(dh * gain_one, normed_one, inv_one)
-    d_bias_out = jnp.sum(dz_one, axis=0)
-    dz_one_low = dz_one.astype(BF)
-    g_out = jnp.einsum("le,ld->ed", attended, dz_one_low, preferred_element_type=F32).astype(BF)
-    g_out = jnp.pad(g_out.reshape(4, 8, 24, 768), ((0, 0), (0, 0), (0, 8), (0, 0))).reshape(4, 256, 768)
-    d_att = jnp.einsum("ld,ed->le", dz_one_low, w_out, preferred_element_type=F32).astype(BF)
-    d_att = d_att.reshape(512, 4, 3, HEAD_DIM)
-    d_prob = jnp.einsum("qthe,tkhe->thqk", d_att, values, preferred_element_type=F32)
-    d_values = jnp.einsum("thqk,qthe->tkhe", prob_low, d_att, preferred_element_type=F32)
-    inner = jnp.sum(d_prob * attn_prob, axis=-1, keepdims=True)
-    d_scores = (attn_prob * (d_prob - inner)).astype(BF)
-    d_queries = jnp.einsum("thqk,tkhe->tqhe", d_scores, keys, preferred_element_type=F32) * scaling
-    d_keys = jnp.einsum("thqk,tqhe->tkhe", d_scores, queries, preferred_element_type=F32) * scaling
-    d_bias_q = jnp.sum(d_queries, axis=1).reshape(4, 192)
-    d_bias_v = jnp.sum(d_values, axis=1).reshape(4, 192)
-    d_qkv = jnp.stack([d_queries, d_keys, d_values], axis=2).astype(BF).reshape(4, 512, 576)
-    g_qkv = jnp.einsum("ld,tle->tde", x_row, d_qkv, preferred_element_type=F32).astype(BF)
-    input_grad = dz_one + jnp.einsum("tle,tde->ld", d_qkv, w_qkv, preferred_element_type=F32)
-
-    shared = jnp.stack([d_bias_out, d_bias_down, d_gain_one, d_shift_one, d_gain_two, d_shift_two])
-    shared = shared.reshape(6, 4, 192).transpose(1, 0, 2).reshape(4, 1152)
-    small_grads = jnp.concatenate([d_bias_q, d_bias_v, d_bias_up, shared], axis=1)
-    small_grads = jnp.pad(small_grads.reshape(4, 1, 18, 128), ((0, 0), (0, 0), (0, 6), (0, 0)))
-    blocks, small_sum, out_mine, dx_mine, pool_all = reduce_call(
-        g_qkv,
-        g_out,
-        g_up,
-        g_down,
-        small_grads,
+    blocks, small_sum, out_mine, dx_mine, pool_all = backward_call(
+        flags.astype(F32)[:, None],
         out_row,
-        input_grad.astype(BF),
         pool_mean,
-    )
-    small_row = small_sum[:18].reshape(block_len)
+        gy_row,
+        normed_two,
+        inverse,
+        small_all,
+        act,
+        pull,
+        w_down,
+        w_up,
+        h_low,
+        normed_one,
+        attended,
+        w_out,
+        qkv,
+        prob_low,
+        w_qkv,
+        x_row,
+    )
+    small_row = small_sum[0]
     norm_grads = small_row[1152:].reshape(6, 192)
     pooled = lax.dynamic_slice_in_dim(pool_all, tensor_at * 192, 192, 2)
 

time: 366 us -> 299 us (0.82)
  matrix products: 52.3 us -> 5.25 us
  local copies, waits for them, and re-layouts: 46.3 us -> 14.7 us
  Pallas kernels: 247 us -> 267 us
  other arithmetic: 15.3 us -> 7.41 us
    dot_general x12 -> x0, matrix products: 47 us -> none  [the longest x1 8.83 us: local_rows(): jnp.einsum('tlf,tdf->ld', d_up_low, w_up, preferred_element_type=F32)]
    pallas_call x1, Pallas kernels: 122 us -> 141 us  [backward_call(): pl.pallas_call(backward_kernel, out_shape=[shape((768, 2304), BF), shape(...]
    reshape x5 -> x0, local copies, waits for them, and re-layouts: 9.49 us -> none  [the longest x1 9.22 us: local_rows(): prob_low = prob_low.reshape(4, 3, 512, 512)]
    convert_element_type x2 -> x1, local copies, waits for them, and re-layouts: 6.27 us -> 0.86 us  [local_rows(): flags.astype(F32)[:, None]]
    reduce_sum x3 -> x0, other arithmetic: 4.7 us -> none  [the longest x1 2.37 us: local_rows(): d_bias_out = jnp.sum(dz_one, axis=0)]
    pallas_call x1 -> x0, local copies, waits for them, and re-layouts: 4.49 us -> none  [forward_call(): pl.pallas_call(forward_kernel, out_shape=[shape(*o) for o in outs], in_sp...]
    another operation x11 -> x0, local copies, waits for them, and re-layouts: 4.18 us -> none  [the longest x3 3.57 us: local_rows(): jnp.stack([d_queries, d_keys, d_values], axis=2).astype(BF)]
    unnamed x60 -> x16, local copies, waits for them, and re-layouts: 7.47 us -> 5.17 us
where the time goes in v1:
time: 299 us; the launch traced here: 295 us
  Pallas kernels  267 us (89%)
  local copies, waits for them, and re-layouts  14.7 us (5%)
  other arithmetic  7.41 us (2%)
  matrix products  5.25 us (2%)
    pallas_call x1, Pallas kernels, backward_call(): pl.pallas_call(backward_kernel, out_shape=[shape((768, 2304), BF), shape(...  141 us
    pallas_call x1, Pallas kernels, forward_call(): pl.pallas_call(forward_kernel, out_shape=[shape(*o) for o in outs], in_sp...  126 us

profile of v1, /device:TPU:9, one launch (start us, length us, event | category | flops | bytes accessed | tf_op | source)
XLA Modules:
  0.0 295.4 jit_solution(189845769406556652)
XLA Ops:
  0.6 0.0 copy-start.1
  0.6 0.0 copy-start.2
  0.7 0.8 compare_bitcast_fusion
  1.5 1.1 convert_reduce_fusion
  2.7 0.7 multiply_add_fusion
  3.3 0.5 slice.28
  3.9 0.7 broadcast_compare_fusion
  4.5 0.2 compare_reduce_fusion
  4.7 0.1 slice.27
  4.8 0.2 fusion.14
  5.1 0.1 reshape.101
  5.1 0.1 reshape.103
  5.2 0.1 reshape.104
  5.3 1.2 broadcast_in_dim.95.small_slot
  6.6 0.1 reshape.102
  6.6 0.1 pad_add_fusion
  6.7 0.1 reshape.105
  6.8 0.1 dynamic_slice.14
  6.9 1.3 compare_select_fusion.1
  8.2 0.2 copy.27
  8.4 0.8 broadcast_in_dim.110.slot_col
  9.2 0.9 copy.32.flag_col
  10.0 0.1 copy.28
  10.2 0.8 subtract_select_fusion.id_col
  10.9 0.0 copy-done.1
  10.9 0.0 copy-done.2
  10.9 1.3 copy_bitcast_fusion
  12.3 125.6 %gather_and_forward.1 = (bf16[4,768,576]{2,1,0:T(8,128)(2,1)}, bf16[4,256,768]{2,1,0:T(8,128)(2,1)}, bf16[4,768,768]{2,1,0:T(8,128)(2,1)}, bf16[4,768,768]{2,1,0...) custom-call(f32[192,2304]{1,0:T(8,128)} %bitcast.36, ...), custom_call_target="tpu_custom_call" | custom-call | tf_op jit(solution)/shard_map/gather_and_forward/pallas_call | solution.py:892
  137.9 141.4 %backward_and_reduce.1 = (bf16[768,2304]{1,0:T(8,128)(2,1)}, f32[8,2304]{1,0:T(8,128)}, bf16[4,128,768]{2,1,0:T(8,128)(2,1)}, bf16[4,128,768]{2,1,0:T(8,128)(2,1)}, f32[4,8,768]{2,1,0:T(8,128)}) custom-call(f32[512,1]{1,0:T(8,128)} %copy.32.flag_col, bf16[512,768]{1,0:T(8,128)(2,1)} %get-tuple-element.30.out_row, f32[8,768]{1,0:T(8,128)} %get-tuple-element.31.pool_in, ...), custom_call_target="tpu_custom_call" | custom-call | tf_op jit(solution)/shard_map/backward_and_reduce/pallas_call | solution.py:1421
  279.3 0.8 slice_reduce_fusion.1
  280.1 0.9 slice_reduce_fusion
  281.0 0.7 reshape.106
  281.7 1.5 constant_dynamic-slice_fusion
  283.2 0.0 copy-start.6
  283.2 1.4 convert_bitcast_fusion.1
  284.6 0.0 copy-start.3
  284.6 0.0 copy-start.5
  284.6 2.2 copy.33
  286.8 0.0 copy-done.3
  286.8 0.0 copy-start.4
  286.8 0.1 convert_bitcast_fusion
  286.9 0.0 copy-start
  286.9 2.2 copy.34
  289.1 0.0 copy-done.6
  289.1 0.0 copy-done.5
  289.1 0.0 copy-done.4
  289.1 0.8 copy-done
  289.9 5.3 %select_bitcast_fusion = (f32[1,192,2304]{2,1,0:T(8,128)}, f32[1,192,2304]{2,1,0:T(8,128)}, f32[1,192,2304]{2,1,0:T(8,128)}) fusion(pred[192]{0:T(512)(128)(4,1)S(1)} %compare_reduce_fusion, f32[1,192,2304]{2,1,0:T(8,128)S(1)} %copy-done.5, f32[1,192,2304]{2,1,0:T(8,128)S(1)} %copy-done.6, s32[192]{0:T(256)S(1)} %broadcast_multiply_fusion, ...), kind=kOutput, calls=%fused_computation.7 | convolution fusion | flops 696434688 | bytes 14169984 | tf_op jit(solution)/shard_map/dot_general | solution.py:455
  (4 shorter events, 0.0 us)
Async XLA Ops:
  0.6 10.3 %copy-start.1 = (bf16[128,4,768]{2,1,0:T(4,128)(2,1)S(1)}, bf16[128,4,768]{2,1,0:T(4,128)(2,1)}, u32[]{:S(2)}) copy-start(bf16[128,4,768]{2,1,0:T(4,128)(2,1)} %param.11) | copy-start | bytes 2359300
  0.6 10.3 %copy-start.2 = (bf16[128,4,768]{2,1,0:T(4,128)(2,1)S(1)}, bf16[128,4,768]{2,1,0:T(4,128)(2,1)}, u32[]{:S(2)}) copy-start(bf16[128,4,768]{2,1,0:T(4,128)(2,1)} %param.8) | copy-start | bytes 2359300
  283.2 5.9 %copy-start.6 = (f32[1,192,2304]{2,1,0:T(8,128)S(1)}, f32[1,192,2304]{2,1,0:T(8,128)}, u32[]{:S(2)}) copy-start(f32[1,192,2304]{2,1,0:T(8,128)} %param.14) | copy-start | bytes 5308420
  284.6 2.2 copy-start.3
  284.6 4.5 %copy-start.5 = (f32[1,192,2304]{2,1,0:T(8,128)S(1)}, f32[1,192,2304]{2,1,0:T(8,128)}, u32[]{:S(2)}) copy-start(f32[1,192,2304]{2,1,0:T(8,128)} %param.15) | copy-start | bytes 5308420
  286.8 2.3 copy-start.4
  286.9 3.0 %copy-start = (f32[1,192,2304]{2,1,0:T(8,128)S(1)}, f32[1,192,2304]{2,1,0:T(8,128)}, u32[]{:S(2)}) copy-start(f32[1,192,2304]{2,1,0:T(8,128)} %param.13) | copy-start | bytes 5308420

commit v2 on v1

--- a/solution.py
+++ b/solution.py
@@ -512,8 +512,10 @@
     row_out,
     pool_out,
     slots,
-    canon,
-    land,
+    canon_att,
+    canon_ffn,
+    land_att,
+    land_ffn,
     share,
     p_qkv,
     p_out,
@@ -549,6 +551,7 @@
 ):
     place = Place()
     link = Sender(send_sems, recv_sems, local_sems)
+    slots[place.c] = master[...].astype(BF)
     place.greet()
     whole = (w_qkv, w_out, w_up, w_down)
     held = (v_qkv, v_out, v_up, v_down)
@@ -557,7 +560,6 @@
     mine_rows = pl.ds(pl.multiple_of(place.t * 128, 128), 128)
     tidy = []
 
-    slots[place.c] = master[...].astype(BF)
     core_slots = link.send(slots.at[place.c], slots.at[place.c], place.core)
     x_moves = [
         link.send(x_in.at[place.ahead[k]], x_row.at[mine_rows], place.deep[k]) for k in (1, 2, 3)
@@ -567,36 +569,47 @@
     core_slots.wait_recv()
 
     pair_slots = slots[...].reshape(384, 2304)
-    slot_id = lax.broadcasted_iota(jnp.int32, (96, 384), 1) + place.xy * 384
-    shares = []
-    order = [(1, place.right), (2, place.down), (3, place.diag), (0, None)]
+    slot_id = lax.broadcasted_iota(jnp.int32, (64, 384), 1) + place.xy * 384
+    order = [(3, place.diag), (1, place.right), (2, place.down), (0, None)]
+
+    def spread(lo, rows, canon, land):
+        sent = []
+        for j, peer in order:
+            at = place.xy if peer is None else peer[0] // 2
+            wanted = slot_col[pl.ds(pl.multiple_of(at * 96 + lo, 32), rows), :]
+            pick = jnp.where(wanted == slot_id[:rows], 1.0, 0.0).astype(BF)
+            canon[j] = dot_f32(pick, pair_slots).astype(BF)
+            if peer is not None:
+                sent.append(link.send(canon.at[j], land.at[j - 1], peer))
+        return sent
+
+    def collect(sent, lo, rows, canon, land):
+        for move in sent:
+            move.wait_recv()
+        share[lo : lo + rows, :] = (
+            canon[0].astype(F32) + land[0].astype(F32) + land[1].astype(F32) + land[2].astype(F32)
+        )
+
+    att_sent = spread(64, 32, canon_att, land_att)
     pick_small = jnp.where(small_slot[...] == slot_id[:8], 1.0, 0.0).astype(BF)
     small_mine[...] = dot_f32(pick_small, pair_slots)
     small_moves = [link.send(small_mine, small_land.at[j], peer) for j, peer in enumerate(peers)]
-    for j, peer in order:
-        at = place.xy if peer is None else peer[0] // 2
-        wanted = slot_col[pl.ds(pl.multiple_of(at * 96, 96), 96), :]
-        pick = jnp.where(wanted == slot_id, 1.0, 0.0).astype(BF)
-        canon[j] = dot_f32(pick, pair_slots).astype(BF)
-        if peer is not None:
-            shares.append(link.send(canon.at[j], land.at[j - 1], peer))
-    for move in shares + small_moves:
-        move.wait_recv()
-    share[...] = (
-        canon[0].astype(F32) + land[0].astype(F32) + land[1].astype(F32) + land[2].astype(F32)
-    )
-    small_total[...] = small_mine[...] + small_land[0] + small_land[1] + small_land[2]
-
-    three = interleave(96, 3)
+    att_sent[0].wait_recv()
+    ffn_sent = spread(0, 64, canon_ffn, land_ffn)
+    collect(att_sent[1:], 64, 32, canon_att, land_att)
+
     p_qkv[...] = dot_f32(
         interleave(96, 4),
         jnp.concatenate([share[64:88, 576 * r : 576 * r + 576] for r in range(4)], axis=0).astype(BF),
     ).astype(BF)
-    out_parts = [share[88:96, 768 * k : 768 * k + 768] for k in range(3)]
-    out_parts = out_parts + [jnp.zeros((8, 768), F32)]
-    p_out[...] = dot_f32(interleave_out(), jnp.concatenate(out_parts, axis=0).astype(BF)).astype(BF)
+
+    def spread_out():
+        parts = [share[88:96, 768 * k : 768 * k + 768] for k in range(3)]
+        parts = parts + [jnp.zeros((8, 768), F32)]
+        p_out[...] = dot_f32(interleave_out(), jnp.concatenate(parts, axis=0).astype(BF)).astype(BF)
 
     def spread_ffn():
+        three = interleave(96, 3)
         for at, ref in ((0, p_up), (32, p_down)):
             parts = [share[at : at + 32, 768 * k : 768 * k + 768] for k in range(3)]
             ref[...] = dot_f32(three, jnp.concatenate(parts, axis=0).astype(BF)).astype(BF)
@@ -651,9 +664,11 @@
             lin = dot_f32(x_row[rows, :], v_qkv[t]) + bias_qkv[t]
             qkv[t, rows, :] = lin.astype(BF)
 
-        row_loop(body)
-
-    def attention(t):
+        row_loop(body, 256)
+
+    def attention(k):
+        t = place.behind[k]
+
         def body(rows):
             allowed = id_col[rows, :] == id_row[...]
             parts = []
@@ -668,7 +683,7 @@
                 parts.append(dot_f32(low, qkv[t, :, 384 + at : 448 + at]))
             att[t, rows, :] = jnp.concatenate(parts, axis=1).astype(BF)
 
-        row_loop(body)
+        row_loop(body, 256)
         tidy.append(link.copy(qkv.at[t], qkv_out.at[t]))
         tidy.append(link.copy(att.at[t], att_out.at[t]))
         tidy.append(link.copy(prob.at[pl.ds(3 * t, 3)], prob_out.at[pl.ds(3 * t, 3)]))
@@ -693,7 +708,7 @@
             h_wide[rows, :] = h
             total[rows, :] = h + norm[1:2, :]
 
-        row_loop(body)
+        row_loop(body, 256)
         tidy.append(link.copy(n_one, n_one_out))
         tidy.append(link.copy(h_low, h_out))
 
@@ -708,7 +723,7 @@
             slope = below + pre * (jnp.exp(-0.5 * pre * pre) * 0.3989422804014327)
             pull[t, rows, :] = slope.astype(BF)
 
-        row_loop(body)
+        row_loop(body, 256)
         tidy.append(link.copy(act.at[t], act_out.at[t]))
         tidy.append(link.copy(pull.at[t], pull_out.at[t]))
 
@@ -719,7 +734,7 @@
         def body(rows):
             total[rows, :] += dot_f32(act[t, rows, :], v_down[t])
 
-        row_loop(body)
+        row_loop(body, 256)
 
     def end_step():
         ids = lax.broadcasted_iota(jnp.int32, (SMAX, 512), 0)
@@ -734,7 +749,7 @@
             h_wide[rows, :] = out
             row_low[rows, :] = out.astype(BF)
 
-        row_loop(body)
+        row_loop(body, 256)
         pool[...] = jnp.dot(member, h_wide[...], precision=exact_precision, preferred_element_type=F32) / count
         tidy.append(link.copy(total, n_two_out))
         tidy.append(link.copy(row_low, row_out))
@@ -742,86 +757,104 @@
         tidy.append(link.copy(inv, inv_out))
 
     every = range(4)
+    others = (1, 2, 3)
     deep_send(0)
+    plane_send(0, 0)
+    spread_out()
     deep_send(1)
-    tidy.append(link.copy(small_total, small.at[place.t]))
-    small_deep = [link.send(small_total, small.at[place.t], place.deep[k]) for k in (1, 2, 3)]
-    plane_send(0, 0)
     plane_send(1, 0)
+    collect(ffn_sent, 0, 64, canon_ffn, land_ffn)
     spread_ffn()
     plane_send(2, 0)
-    for k in (1, 2, 3):
+    plane_pass(0, 0)
+    for k in others:
         plane_send(0, k)
     deep_send(2)
+    for move in small_moves:
+        move.wait_recv()
+    small_total[...] = small_mine[...] + small_land[0] + small_land[1] + small_land[2]
+    small_stay = link.copy(small_total, small.at[place.t])
+    small_deep = [link.send(small_total, small.at[place.t], place.deep[k]) for k in others]
+    x_stay.wait()
+    for move in x_moves:
+        move.wait_recv()
+    tidy.append(link.copy(x_row, x_out))
+    plane_pass(1, 0)
+    for k in others:
+        plane_send(1, k)
+    core_pass(0, 0)
     plane_send(3, 0)
-    for k in every:
+    for k in others:
         plane_pass(0, k)
-    for k in (1, 2, 3):
-        plane_send(1, k)
+    small_stay.wait()
     for move in small_deep:
         move.wait_recv()
-    tidy.pop().wait()
     norm_vectors(small, norm)
     for t in every:
         bias_qkv[t] = jnp.concatenate(
             [small[t, 0:1, :192], jnp.zeros((1, 192), F32), small[t, 0:1, 192:384]], axis=1
         )
     tidy.append(link.copy(small, small_out))
-    x_stay.wait()
-    for move in x_moves:
-        move.wait_recv()
-    tidy.append(link.copy(x_row, x_out))
-    for k in every:
-        core_pass(0, k)
-    for k in every:
-        plane_pass(1, k)
-    for k in every:
-        load(0, k)
-    for k in (1, 2, 3):
+    load(0, 0)
+    qkv_step(0)
+    attention(0)
+    for k in others:
         plane_send(2, k)
     deep_send(3)
-    gy_moves = [
-        link.send(gy_in.at[place.ahead[k]], gy_row.at[mine_rows], place.deep[k]) for k in (1, 2, 3)
-    ]
-    for k in every:
-        qkv_step(k)
+    for k in others:
+        plane_pass(1, k)
+        core_pass(0, k)
+    plane_pass(2, 0)
+    for k in others:
+        load(0, k)
+    qkv_step(1)
+    attention(1)
+    plane_pass(3, 0)
     for k in every:
         core_pass(1, k)
-    plane_pass(2, 0)
     plane_pass(2, 1)
+    qkv_step(2)
+    attention(2)
+    plane_pass(2, 2)
+    core_pass(2, 0)
     for k in every:
         load(1, k)
-    attention(0)
-    plane_pass(2, 2)
+    qkv_step(3)
     plane_pass(2, 3)
-    for k in (1, 2, 3):
-        plane_send(3, k)
-    attention(1)
-    for k in every:
-        core_pass(2, k)
-    attention(2)
-    for k in every:
-        load(2, k)
-    plane_pass(3, 0)
+    core_pass(2, 1)
     attention(3)
+    load(2, 0)
+    plane_send(3, 1)
+    plane_send(3, 2)
+    plane_send(3, 3)
+    gy_moves = [
+        link.send(gy_in.at[place.ahead[k]], gy_row.at[mine_rows], place.deep[k]) for k in others
+    ]
+    core_pass(2, 2)
+    core_pass(3, 0)
+    out_step()
+    load(2, 1)
+    load(2, 2)
+    load(3, 0)
+    core_pass(2, 3)
     plane_pass(3, 1)
-    out_step()
+    up_step(0)
+    up_step(1)
     plane_pass(3, 2)
+    core_pass(3, 1)
+    load(2, 3)
+    load(3, 1)
+    up_step(2)
     plane_pass(3, 3)
-    core_pass(3, 0)
-    up_step(0)
-    core_pass(3, 1)
-    load(3, 0)
-    up_step(1)
     core_pass(3, 2)
+    up_step(3)
+    down_step(0)
     core_pass(3, 3)
-    up_step(2)
-    load(3, 1)
-    up_step(3)
+    down_step(1)
     load(3, 2)
+    down_step(2)
     load(3, 3)
-    for k in every:
-        down_step(k)
+    down_step(3)
     end_step()
     for move in gy_moves:
         move.wait_recv()
@@ -857,8 +890,10 @@
     ]
     scratch = [
         ((2, 192, 2304), BF),
-        ((4, 96, 2304), BF),
-        ((3, 96, 2304), BF),
+        ((4, 32, 2304), BF),
+        ((4, 64, 2304), BF),
+        ((3, 32, 2304), BF),
+        ((3, 64, 2304), BF),
         ((96, 2304), F32),
         ((96, 576), BF),
         ((32, 768), BF),
@@ -1128,7 +1163,7 @@
         got["act", i].wait()
         produce(3, k, lambda which: dot_tn(act[slot, :, lanes(which)], low[...]))
 
-    def up_piece(i):
+    def act_back(i):
         k, slot = steps[i], i % 2
         got["down", i].wait()
         got["pull", i].wait()
@@ -1139,9 +1174,11 @@
             d_up[rows, :] = grad.astype(BF)
 
         row_loop(body, 256)
+
+    def up_piece(i):
         if i == 0:
             got["h"].wait()
-        produce(2, k, lambda which: dot_tn(h_low[:, lanes(which)], d_up[...]))
+        produce(2, steps[i], lambda which: dot_tn(h_low[:, lanes(which)], d_up[...]))
 
     def hidden_back(i):
         slot = i % 2
@@ -1238,6 +1275,31 @@
         if i + 2 < 4:
             load_att(i + 2)
 
+    def share_send(lo, hi):
+        share_low[lo:hi, :] = share[lo:hi, :].astype(BF)
+        mine = c * 4 + place.xy
+        rows = pl.ds(lo, hi - lo)
+        return (
+            link.copy(share_low.at[rows], blocks.at[mine, rows]),
+            link.send(share_low.at[rows], blocks.at[mine, rows], place.right),
+            link.send(share_low.at[rows], blocks.at[mine, rows], place.down),
+        )
+
+    def share_pass(sent, lo, hi):
+        half = (hi - lo) // 2
+        sent[1].wait_recv()
+        sent[2].wait_recv()
+        one = blocks.at[c * 4 + place.right[0] // 2, pl.ds(lo, half)]
+        two = blocks.at[c * 4 + place.down[0] // 2, pl.ds(lo + half, half)]
+        return link.send(one, one, place.down), link.send(two, two, place.right)
+
+    def share_across(sent, passed, lo, hi):
+        sent[0].wait()
+        passed[0].wait_recv()
+        passed[1].wait_recv()
+        spot = blocks.at[pl.ds(c * 4, 4), pl.ds(lo, hi - lo)]
+        return link.send(spot, spot, place.core)
+
     got["small"].wait()
     norm_vectors(small, norm)
     reds[...] = jnp.zeros_like(reds)
@@ -1247,78 +1309,91 @@
     for name in ("normed", "gy", "inv"):
         got[name].wait()
     norm_two_back()
-    a, b, d, e = ((3, k) for k in steps)
-    f, g, h, j = ((2, k) for k in steps)
+    down = [(3, k) for k in steps]
+    up = [(2, k) for k in steps]
+    out = [(1, k) for k in steps]
+    att_in_w = [(0, k) for k in steps]
     down_piece(0)
+    act_back(0)
+    core_add(*down[0])
     up_piece(0)
-    core_add(*a)
     hidden_back(0)
-    core_add(*f)
+    core_add(*up[0])
+    plane_add(*down[0])
     down_piece(1)
-    plane_add(*a)
+    act_back(1)
+    core_add(*down[1])
+    plane_add(*up[0])
     up_piece(1)
-    core_add(*b)
+    deep_add(*down[0])
     hidden_back(1)
-    core_add(*g)
-    plane_add(*f)
+    core_add(*up[1])
+    plane_add(*down[1])
     down_piece(2)
-    deep_add(*a)
-    core_add(*d)
+    deep_add(*up[0])
+    act_back(2)
+    core_add(*down[2])
     up_piece(2)
-    plane_add(*b)
-    deep_add(*f)
+    plane_add(*up[1])
+    deep_add(*down[1])
     hidden_back(2)
-    core_add(*h)
+    core_add(*up[2])
     down_piece(3)
-    core_add(*e)
+    plane_add(*down[2])
+    deep_add(*up[1])
+    act_back(3)
+    core_add(*down[3])
     up_piece(3)
-    plane_add(*g)
-    deep_add(*b)
+    deep_add(*down[2])
     hidden_back(3)
-    core_add(*j)
+    core_add(*up[3])
+    plane_add(*up[2])
     norm_one_back()
-    plane_add(*d)
-    deep_add(*g)
     out_piece(0)
+    plane_add(*down[3])
+    deep_add(*up[2])
     attention_back(0)
-    plane_add(*h)
-    deep_add(*d)
-    core_add(1, 1)
+    core_add(*out[0])
+    plane_add(*up[3])
+    deep_add(*down[3])
     qkv_piece(0)
-    plane_add(*e)
-    deep_add(*h)
-    core_add(0, 1)
     out_piece(1)
+    deep_add(*up[3])
+    core_add(*att_in_w[0])
     attention_back(1)
-    core_add(1, 2)
+    core_add(*out[1])
+    plane_add(*out[0])
+    end(3)
+    end(2)
+    ffn_sent = share_send(0, 64)
     qkv_piece(1)
-    plane_add(*j)
-    deep_add(*e)
-    core_add(0, 2)
+    plane_add(*att_in_w[0])
+    deep_add(*out[0])
     out_piece(2)
+    core_add(*att_in_w[1])
     attention_back(2)
-    core_add(1, 3)
-    deep_add(*j)
-    plane_add(1, 1)
+    core_add(*out[2])
+    plane_add(*out[1])
+    deep_add(*att_in_w[0])
+    ffn_passed = share_pass(ffn_sent, 0, 64)
     qkv_piece(2)
-    core_add(0, 3)
-    plane_add(0, 1)
-    deep_add(1, 1)
+    plane_add(*att_in_w[1])
     out_piece(3)
+    core_add(*att_in_w[2])
+    deep_add(*out[1])
     attention_back(3)
-    core_add(1, 0)
+    core_add(*out[3])
+    plane_add(*out[2])
+    deep_add(*att_in_w[1])
     qkv_piece(3)
-    core_add(0, 0)
+    plane_add(*att_in_w[2])
+    plane_add(*out[3])
+    core_add(*att_in_w[3])
 
     def dx_body(rows):
         low[rows, :] = total[rows, :].astype(BF)
 
     row_loop(dx_body)
-    own_rows = pl.ds(pl.multiple_of(t * 128, 128), 128)
-    stay.append(link.copy(low.at[own_rows], dx_mine.at[t]))
-    for k in (1, 2, 3):
-        part = low.at[pl.ds(pl.multiple_of(t_of[k] * 128, 128), 128)]
-        moves.append(link.send(part, dx_mine.at[t], place.deep[k]))
     for q in range(4):
         at = slice(192 * q, 192 * q + 192)
         small_grad[q, 0:1, :] = jnp.concatenate(
@@ -1327,46 +1402,38 @@
     small_sum = small_land.at[6]
     small_keep = link.copy(small_grad.at[t], small_sum)
     small_moves = [link.send(small_grad.at[t_of[k]], small_land.at[k - 1], place.deep[k]) for k in (1, 2, 3)]
-    plane_add(1, 2)
-    deep_add(0, 1)
-    plane_add(0, 2)
-    deep_add(1, 2)
-    plane_add(1, 3)
-    deep_add(0, 2)
-    plane_add(0, 3)
-    deep_add(1, 3)
-    end(3)
-    end(2)
-    plane_add(1, 0)
-    plane_add(0, 0)
-    deep_add(0, 3)
-    deep_add(1, 0)
-    deep_add(0, 0)
-    end(1)
+
+    deep_add(*out[2])
+    deep_add(*att_in_w[2])
+    own_rows = pl.ds(pl.multiple_of(t * 128, 128), 128)
+    stay.append(link.copy(low.at[own_rows], dx_mine.at[t]))
+    for k in (1, 2, 3):
+        part = low.at[pl.ds(pl.multiple_of(t_of[k] * 128, 128), 128)]
+        moves.append(link.send(part, dx_mine.at[t], place.deep[k]))
     small_keep.wait()
     for move in small_moves:
         move.wait_recv()
     small_land[7] = small_land[6] + small_land[0] + small_land[1] + small_land[2]
-    for i, peer in enumerate((place.core, place.right, place.down)):
-        move = link.send(small_land.at[7 + i], small_land.at[3 + i], peer)
-        if i == 1:
-            end(0)
-            share_low[...] = share[...].astype(BF)
-            dest = pl.ds(pl.multiple_of((c * 4 + place.xy) * 96, 96), 96)
-            kept = link.copy(share_low, blocks.at[dest])
-            last = [
-                link.send(share_low, blocks.at[dest], to)
-                for to in (place.diag, place.right, place.down)
-            ]
-        move.wait_recv()
-        small_land[8 + i] = small_land[7 + i] + small_land[3 + i]
-    small_out[...] = small_land[10]
-    kept.wait()
-    for move in last:
-        move.wait_recv()
-    half = pl.ds(pl.multiple_of(c * 384, 384), 384)
-    across = link.send(blocks.at[half], blocks.at[half], place.core)
-    across.wait_recv()
+    doubling = [link.send(small_land.at[7], small_land.at[3], place.core)]
+    deep_add(*out[3])
+    plane_add(*att_in_w[3])
+    ffn_across = share_across(ffn_sent, ffn_passed, 0, 64)
+    deep_add(*att_in_w[3])
+    end(1)
+    doubling[0].wait_recv()
+    small_land[8] = small_land[7] + small_land[3]
+    doubling.append(link.send(small_land.at[8], small_land.at[4], place.right))
+    end(0)
+    att_sent = share_send(64, 96)
+    doubling[1].wait_recv()
+    small_land[9] = small_land[8] + small_land[4]
+    doubling.append(link.send(small_land.at[9], small_land.at[5], place.down))
+    att_passed = share_pass(att_sent, 64, 96)
+    doubling[2].wait_recv()
+    small_out[...] = small_land[9] + small_land[5]
+    att_across = share_across(att_sent, att_passed, 64, 96)
+    ffn_across.wait_recv()
+    att_across.wait_recv()
     for move in moves:
         move.wait_recv()
     for copy in stay:
@@ -1421,7 +1488,7 @@
     return pl.pallas_call(
         backward_kernel,
         out_shape=[
-            shape((768, 2304), BF),
+            shape((8, 96, 2304), BF),
             shape((8, 2304), F32),
             shape((4, 128, 768), BF),
             shape((4, 128, 768), BF),
@@ -1529,7 +1596,7 @@
     wanted = data_at * per_owner + jnp.arange(per_owner, dtype=jnp.int32)
     block_of, filled = slot_blocks(slot_of, wanted)
     pick = (slot_order[None, :] == wanted[:, None]).astype(BF)
-    owned = dot_f32(pick, blocks)
+    owned = dot_f32(pick, blocks.reshape(768, block_len))
     owned = jnp.where((wanted == slot_of[768])[:, None], small_row[None], owned)
     token_position = block_of[:, None] * block_len + jnp.arange(block_len, dtype=jnp.int32)[None, :]
     step_rate, decay_on = step_rates(token_position, MODEL_WIDTH, FF, 4)

time: 299 us -> 263 us (0.88)
  Pallas kernels: 267 us -> 230 us
    pallas_call x1, Pallas kernels: 141 us -> 116 us  [backward_call(): pl.pallas_call(backward_kernel, out_shape=[shape((8, 96, 2304), BF), shap...]
    pallas_call x1, Pallas kernels: 126 us -> 114 us  [forward_call(): pl.pallas_call(forward_kernel, out_shape=[shape(*o) for o in outs], in_sp...]
where the time goes in v2:
time: 263 us; the launch traced here: 259 us
  Pallas kernels  230 us (87%)
  local copies, waits for them, and re-layouts  14.7 us (6%)
  other arithmetic  7.41 us (3%)
  matrix products  5.25 us (2%)
    pallas_call x1, Pallas kernels, backward_call(): pl.pallas_call(backward_kernel, out_shape=[shape((8, 96, 2304), BF), shap...  116 us
    pallas_call x1, Pallas kernels, forward_call(): pl.pallas_call(forward_kernel, out_shape=[shape(*o) for o in outs], in_sp...  114 us

profile of v2, /device:TPU:9, one launch (start us, length us, event | category | flops | bytes accessed | tf_op | source)
XLA Modules:
  0.0 258.7 jit_solution(14978262260911133748)
XLA Ops:
  0.6 0.0 copy-start.1
  0.6 0.0 copy-start.2
  0.7 0.8 compare_bitcast_fusion
  1.5 1.1 convert_reduce_fusion
  2.7 0.7 multiply_add_fusion
  3.3 0.5 slice.28
  3.9 0.7 broadcast_compare_fusion
  4.5 0.2 compare_reduce_fusion
  4.7 0.1 slice.27
  4.8 0.2 fusion.14
  5.1 0.1 reshape.104
  5.1 0.1 reshape.106
  5.2 0.1 reshape.107
  5.3 1.2 broadcast_in_dim.95.small_slot
  6.6 0.1 reshape.105
  6.6 0.1 pad_add_fusion
  6.7 0.1 reshape.108
  6.8 0.1 dynamic_slice.14
  6.9 1.3 compare_select_fusion.1
  8.2 0.2 copy.27
  8.4 0.8 broadcast_in_dim.110.slot_col
  9.2 0.9 copy.32.flag_col
  10.0 0.1 copy.28
  10.2 0.8 subtract_select_fusion.id_col
  10.9 0.0 copy-done.1
  10.9 0.0 copy-done.2
  10.9 1.3 copy_bitcast_fusion
  12.3 114.1 %gather_and_forward.1 = (bf16[4,768,576]{2,1,0:T(8,128)(2,1)}, bf16[4,256,768]{2,1,0:T(8,128)(2,1)}, bf16[4,768,768]{2,1,0:T(8,128)(2,1)}, bf16[4,768,768]{2,1,0...) custom-call(f32[192,2304]{1,0:T(8,128)} %bitcast.37, ...), custom_call_target="tpu_custom_call" | custom-call | tf_op jit(solution)/shard_map/gather_and_forward/pallas_call | solution.py:927
  126.4 116.0 %backward_and_reduce.1 = (bf16[8,96,2304]{2,1,0:T(8,128)(2,1)}, f32[8,2304]{1,0:T(8,128)}, bf16[4,128,768]{2,1,0:T(8,128)(2,1)}, bf16[4,128,768]{2,1,0:T(8,128)(2,1)}, f32[4,8,768]{2,1,0:T(8,128)}) custom-call(f32[512,1]{1,0:T(8,128)} %copy.32.flag_col, bf16[512,768]{1,0:T(8,128)(2,1)} %get-tuple-element.30.out_row, f32[8,768]{1,0:T(8,128)} %get-tuple-element.31.pool_in, ...), custom_call_target="tpu_custom_call" | custom-call | tf_op jit(solution)/shard_map/backward_and_reduce/pallas_call | solution.py:1488
  242.4 0.8 slice_reduce_fusion.1
  243.2 0.9 slice_reduce_fusion
  244.1 0.7 reshape.110
  244.7 1.5 constant_dynamic-slice_fusion
  246.2 0.0 copy-start.6
  246.2 1.4 convert_bitcast_fusion.1
  247.6 0.0 copy-start.3
  247.6 0.0 copy-start.5
  247.7 2.2 copy.33
  249.8 0.0 copy-done.3
  249.8 0.0 copy-start.4
  249.8 0.1 convert_bitcast_fusion
  250.0 0.0 copy-start
  250.0 2.2 copy.34
  252.1 0.0 copy-done.6
  252.1 0.0 copy-done.5
  252.1 0.0 copy-done.4
  252.1 0.8 copy-done
  253.0 5.2 %select_bitcast_fusion = (f32[1,192,2304]{2,1,0:T(8,128)}, f32[1,192,2304]{2,1,0:T(8,128)}, f32[1,192,2304]{2,1,0:T(8,128)}) fusion(pred[192]{0:T(512)(128)(4,1)S(1)} %compare_reduce_fusion, f32[1,192,2304]{2,1,0:T(8,128)S(1)} %copy-done.5, f32[1,192,2304]{2,1,0:T(8,128)S(1)} %copy-done.6, s32[192]{0:T(256)S(1)} %broadcast_multiply_fusion, ...), kind=kOutput, calls=%fused_computation.7 | convolution fusion | flops 696434688 | bytes 14169984 | tf_op jit(solution)/shard_map/dot_general | solution.py:455
  (4 shorter events, 0.0 us)
Async XLA Ops:
  0.6 10.3 %copy-start.1 = (bf16[128,4,768]{2,1,0:T(4,128)(2,1)S(1)}, bf16[128,4,768]{2,1,0:T(4,128)(2,1)}, u32[]{:S(2)}) copy-start(bf16[128,4,768]{2,1,0:T(4,128)(2,1)} %param.11) | copy-start | bytes 2359300
  0.6 10.3 %copy-start.2 = (bf16[128,4,768]{2,1,0:T(4,128)(2,1)S(1)}, bf16[128,4,768]{2,1,0:T(4,128)(2,1)}, u32[]{:S(2)}) copy-start(bf16[128,4,768]{2,1,0:T(4,128)(2,1)} %param.8) | copy-start | bytes 2359300
  246.2 5.9 %copy-start.6 = (f32[1,192,2304]{2,1,0:T(8,128)S(1)}, f32[1,192,2304]{2,1,0:T(8,128)}, u32[]{:S(2)}) copy-start(f32[1,192,2304]{2,1,0:T(8,128)} %param.14) | copy-start | bytes 5308420
  247.6 2.2 copy-start.3
  247.6 4.5 %copy-start.5 = (f32[1,192,2304]{2,1,0:T(8,128)S(1)}, f32[1,192,2304]{2,1,0:T(8,128)}, u32[]{:S(2)}) copy-start(f32[1,192,2304]{2,1,0:T(8,128)} %param.15) | copy-start | bytes 5308420
  249.8 2.3 copy-start.4
  250.0 3.0 %copy-start = (f32[1,192,2304]{2,1,0:T(8,128)S(1)}, f32[1,192,2304]{2,1,0:T(8,128)}, u32[]{:S(2)}) copy-start(f32[1,192,2304]{2,1,0:T(8,128)} %param.13) | copy-start | bytes 5308420

commit v3 on v2

--- a/solution.py
+++ b/solution.py
@@ -1,5 +1,5 @@
 import jax
-import functools
+import numpy as np
 import jax.numpy as jnp
 from jax import lax
 from jax.experimental import pallas as pl
@@ -472,6 +472,11 @@
     return lax.dot_general(a, b, (((0,), (0,)), ((), ())), preferred_element_type=F32)
 
 
+def unpack_small(packed, small):
+    for t in range(4):
+        small[t] = jnp.concatenate([packed[t, i : i + 1, :] for i in range(6)], axis=1)
+
+
 def norm_vectors(small, norm):
     for i in range(6):
         at = 1152 + 192 * i
@@ -486,10 +491,10 @@
 
 def forward_kernel(
     master,
-    slot_col,
-    small_slot,
-    id_col,
-    id_row,
+    owners,
+    order_col,
+    labels,
+    flags,
     x_in,
     gy_in,
     w_qkv,
@@ -497,6 +502,7 @@
     w_up,
     w_down,
     out_compact,
+    slot_out,
     small_out,
     x_out,
     gy_row,
@@ -511,11 +517,17 @@
     inv_out,
     row_out,
     pool_out,
+    slot_row,
+    slot_col,
+    id_row,
+    id_col,
     slots,
     canon_att,
     canon_ffn,
     land_att,
     land_ffn,
+    pass_ffn,
+    pass_land,
     share,
     p_qkv,
     p_out,
@@ -524,6 +536,7 @@
     small_mine,
     small_land,
     small_total,
+    packed,
     small,
     norm,
     bias_qkv,
@@ -552,13 +565,38 @@
     place = Place()
     link = Sender(send_sems, recv_sems, local_sems)
     slots[place.c] = master[...].astype(BF)
+
+    blocks = owners.shape[1]
+    wide = slot_row.shape[1]
+    owner = jnp.concatenate(
+        [owners[...].astype(F32), jnp.full((1, wide - blocks), -1.0, F32)], axis=1
+    )
+    kinds = lax.broadcasted_iota(jnp.int32, (8, wide), 0).astype(F32)
+    owned = jnp.where(kinds == owner, 1.0, 0.0)
+    ordinal = lax.broadcasted_iota(jnp.int32, (wide, wide), 1)
+    earlier = jnp.where(lax.broadcasted_iota(jnp.int32, (wide, wide), 0) < ordinal, 1.0, 0.0)
+    ahead = dot_f32(owned.astype(BF), earlier.astype(BF))
+    ranking = jnp.sum(owned * ahead, axis=0, keepdims=True)
+    place_of = jnp.where(order_col[...] == ordinal, 1.0, 0.0).astype(BF)
+    pair = jnp.where(kinds == 0.0, owner, ranking).astype(BF)
+    row = dot_nt(pair, place_of)
+    col = dot_nt(place_of, pair)
+    per_owner = float(master.shape[0])
+    slot_row[...] = jnp.broadcast_to(row[0:1, :] * per_owner + row[1:2, :], slot_row.shape)
+    slot_col[...] = jnp.broadcast_to(col[:, 0:1] * per_owner + col[:, 1:2], slot_col.shape)
+
+    own = pl.ds(place.t, 1)
+    apart = -1 - lax.broadcasted_iota(jnp.int32, (1, 512), 1)
+    ids = jnp.where(flags[own, :] == 1, labels[own, :], apart).astype(F32)
+    id_row[...] = jnp.broadcast_to(ids, id_row.shape)
+    id_col[...] = jnp.transpose(id_row[...])
     place.greet()
     whole = (w_qkv, w_out, w_up, w_down)
     held = (v_qkv, v_out, v_up, v_down)
     piece = (p_qkv, p_out, p_up, p_down)
     peers = (place.right, place.down, place.diag)
     mine_rows = pl.ds(pl.multiple_of(place.t * 128, 128), 128)
-    tidy = []
+    tidy = [link.copy(slot_row, slot_out)]
 
     core_slots = link.send(slots.at[place.c], slots.at[place.c], place.core)
     x_moves = [
@@ -569,14 +607,15 @@
     core_slots.wait_recv()
 
     pair_slots = slots[...].reshape(384, 2304)
-    slot_id = lax.broadcasted_iota(jnp.int32, (64, 384), 1) + place.xy * 384
+    slot_id = (lax.broadcasted_iota(jnp.int32, (64, 384), 1) + place.xy * 384).astype(F32)
     order = [(3, place.diag), (1, place.right), (2, place.down), (0, None)]
 
     def spread(lo, rows, canon, land):
         sent = []
         for j, peer in order:
             at = place.xy if peer is None else peer[0] // 2
-            wanted = slot_col[pl.ds(pl.multiple_of(at * 96 + lo, 32), rows), :]
+            spot = pl.ds(pl.multiple_of(place.c * 384 + at * 96 + lo, 32), rows)
+            wanted = slot_col[spot, 0:1]
             pick = jnp.where(wanted == slot_id[:rows], 1.0, 0.0).astype(BF)
             canon[j] = dot_f32(pick, pair_slots).astype(BF)
             if peer is not None:
@@ -591,11 +630,46 @@
         )
 
     att_sent = spread(64, 32, canon_att, land_att)
-    pick_small = jnp.where(small_slot[...] == slot_id[:8], 1.0, 0.0).astype(BF)
-    small_mine[...] = dot_f32(pick_small, pair_slots)
+    pick_small = jnp.where(slot_row[:, 768:769] == slot_id[:8], 1.0, 0.0).astype(BF)
+    picked = dot_f32(pick_small, pair_slots)
+    for i in range(6):
+        small_mine[i : i + 1, :] = picked[0:1, 384 * i : 384 * i + 384]
+    small_mine[6:8, :] = jnp.zeros((2, 384), F32)
     small_moves = [link.send(small_mine, small_land.at[j], peer) for j, peer in enumerate(peers)]
+    def spread_halves():
+        for j, peer in order:
+            at = place.xy if peer is None else peer[0] // 2
+            spot = pl.ds(pl.multiple_of(place.c * 384 + at * 96, 32), 64)
+            pick = jnp.where(slot_col[spot, 0:1] == slot_id, 1.0, 0.0).astype(BF)
+            canon_ffn[j] = dot_f32(pick, pair_slots).astype(BF)
+            if j in (1, 3):
+                half = canon_ffn.at[j, pl.ds(0, 32)]
+                halves[j, 0] = link.send(half, land_ffn.at[0, j // 2], place.right)
+            if j in (2, 3):
+                half = canon_ffn.at[j, pl.ds(32, 32)]
+                halves[j, 1] = link.send(half, land_ffn.at[1, j - 2], place.down)
+
+    def pass_halves():
+        halves[3, 0].wait_recv()
+        pass_ffn[0] = canon_ffn[2, 0:32, :] + land_ffn[0, 1]
+        halves["down"] = link.send(pass_ffn.at[0], pass_land.at[0], place.down)
+        halves[3, 1].wait_recv()
+        pass_ffn[1] = canon_ffn[1, 32:64, :] + land_ffn[1, 1]
+        halves["right"] = link.send(pass_ffn.at[1], pass_land.at[1], place.right)
+
+    def collect_halves():
+        halves[1, 0].wait_recv()
+        halves[2, 1].wait_recv()
+        halves["down"].wait_recv()
+        halves["right"].wait_recv()
+        for i in range(2):
+            share[32 * i : 32 * i + 32, :] = (
+                canon_ffn[0, 32 * i : 32 * i + 32, :] + land_ffn[i, 0] + pass_land[i]
+            ).astype(F32)
+
+    halves = {}
     att_sent[0].wait_recv()
-    ffn_sent = spread(0, 64, canon_ffn, land_ffn)
+    spread_halves()
     collect(att_sent[1:], 64, 32, canon_att, land_att)
 
     p_qkv[...] = dot_f32(
@@ -670,7 +744,7 @@
         t = place.behind[k]
 
         def body(rows):
-            allowed = id_col[rows, :] == id_row[...]
+            allowed = id_col[rows, 0:1] == id_row[0:1, :]
             parts = []
             for i in range(3):
                 at = 64 * i
@@ -737,8 +811,8 @@
         row_loop(body, 256)
 
     def end_step():
-        ids = lax.broadcasted_iota(jnp.int32, (SMAX, 512), 0)
-        member = jnp.where(ids == id_row[...], 1.0, 0.0)
+        sentence = lax.broadcasted_iota(jnp.int32, (SMAX, 512), 0).astype(F32)
+        member = jnp.where(sentence == id_row[...], 1.0, 0.0)
         count = jnp.maximum(jnp.sum(member, axis=1, keepdims=True), 1.0)
 
         def body(rows):
@@ -763,7 +837,8 @@
     spread_out()
     deep_send(1)
     plane_send(1, 0)
-    collect(ffn_sent, 0, 64, canon_ffn, land_ffn)
+    pass_halves()
+    collect_halves()
     spread_ffn()
     plane_send(2, 0)
     plane_pass(0, 0)
@@ -773,8 +848,8 @@
     for move in small_moves:
         move.wait_recv()
     small_total[...] = small_mine[...] + small_land[0] + small_land[1] + small_land[2]
-    small_stay = link.copy(small_total, small.at[place.t])
-    small_deep = [link.send(small_total, small.at[place.t], place.deep[k]) for k in others]
+    small_stay = link.copy(small_total, packed.at[place.t])
+    small_deep = [link.send(small_total, packed.at[place.t], place.deep[k]) for k in others]
     x_stay.wait()
     for move in x_moves:
         move.wait_recv()
@@ -789,12 +864,13 @@
     small_stay.wait()
     for move in small_deep:
         move.wait_recv()
+    unpack_small(packed, small)
     norm_vectors(small, norm)
     for t in every:
         bias_qkv[t] = jnp.concatenate(
             [small[t, 0:1, :192], jnp.zeros((1, 192), F32), small[t, 0:1, 192:384]], axis=1
         )
-    tidy.append(link.copy(small, small_out))
+    tidy.append(link.copy(packed, small_out))
     load(0, 0)
     qkv_step(0)
     attention(0)
@@ -863,7 +939,7 @@
     link.finish()
 
 
-def forward_call(master, slot_col, small_slot, id_col, id_row, x_in, gy_in):
+def forward_call(master, owners, order_col, labels, flags, x_in, gy_in):
     anywhere = pl.BlockSpec(memory_space=pl.ANY)
     vmem = pl.BlockSpec(memory_space=pltpu.VMEM)
     shape = jax.ShapeDtypeStruct
@@ -873,7 +949,8 @@
         ((4, 768, 768), BF),
         ((4, 768, 768), BF),
         ((4, 192, 768), BF),
-        ((4, 8, 2304), F32),
+        ((8, 896), F32),
+        ((4, 8, 384), F32),
         ((512, 768), BF),
         ((512, 768), BF),
         ((4, 512, 576), BF),
@@ -889,20 +966,27 @@
         ((8, 768), F32),
     ]
     scratch = [
+        ((8, 896), F32),
+        ((896, 8), F32),
+        ((8, 512), F32),
+        ((512, 8), F32),
         ((2, 192, 2304), BF),
         ((4, 32, 2304), BF),
         ((4, 64, 2304), BF),
         ((3, 32, 2304), BF),
-        ((3, 64, 2304), BF),
+        ((2, 2, 32, 2304), BF),
+        ((2, 32, 2304), BF),
+        ((2, 32, 2304), BF),
         ((96, 2304), F32),
         ((96, 576), BF),
         ((32, 768), BF),
         ((96, 768), BF),
         ((96, 768), BF),
-        ((8, 2304), F32),
-        ((3, 8, 2304), F32),
-        ((8, 2304), F32),
-        ((4, 8, 2304), F32),
+        ((8, 384), F32),
+        ((3, 8, 384), F32),
+        ((8, 384), F32),
+        ((4, 8, 384), F32),
+        ((4, 1, 2304), F32),
         ((8, 768), F32),
         ((4, 1, 576), F32),
         ((4, 768, 576), BF),
@@ -931,19 +1015,19 @@
         out_specs=[anywhere] * len(outs),
         scratch_shapes=[pltpu.VMEM(*s) for s in scratch]
         + [
-            pltpu.SemaphoreType.DMA((112,)),
-            pltpu.SemaphoreType.DMA((112,)),
+            pltpu.SemaphoreType.DMA((128,)),
+            pltpu.SemaphoreType.DMA((128,)),
             pltpu.SemaphoreType.DMA((64,)),
         ],
         compiler_params=pltpu.CompilerParams(
             collective_id=0, has_side_effects=True, vmem_limit_bytes=60 * MIB
         ),
         name="gather_and_forward",
-    )(master, slot_col, small_slot, id_col, id_row, x_in, gy_in)
+    )(master, owners, order_col, labels, flags, x_in, gy_in)
 
 
 def backward_kernel(
-    flag_col,
+    flags,
     out_row,
     pool_in,
     gy_in,
@@ -977,6 +1061,7 @@
         share_low,
         small_grad,
         small_land,
+        packed,
         small,
         norm,
         gy,
@@ -1004,6 +1089,7 @@
         reds,
         red_up,
         red_qv,
+        flag_col,
         send_sems,
         recv_sems,
         local_sems,
@@ -1017,7 +1103,7 @@
     def load(name, src, dst):
         got[name] = link.copy(src, dst)
 
-    load("small", small_in, small)
+    load("small", small_in, packed)
     load("normed", n_two_in, normed)
     load("gy", gy_in, gy)
     load("inv", inv_in, inv)
@@ -1034,15 +1120,8 @@
         load(("prob", i), prob_in.at[pl.ds(3 * t, 3)], prob.at[slot])
         load(("qkv", i), w_qkv.at[t], v_qkv.at[slot])
 
-    load_ffn(0)
-    load("h", h_in, h_low)
-    load_ffn(1)
-    load("att", att_in, att)
-    load("wout", w_out, v_out)
-    load("qkvs", qkv_in, qkv)
-    load("x", x_in, x_row)
-    load_att(0)
-    load_att(1)
+    own_flags = flags[pl.ds(place.t, 1), :].astype(F32)
+    flag_col[...] = jnp.transpose(jnp.broadcast_to(own_flags, (8, 512)))
     place.greet()
     t, x, y, c = place.t, place.x, place.y, place.c
 
@@ -1143,7 +1222,7 @@
 
     def norm_two_back():
         def body(rows):
-            grad = gy[rows, :].astype(F32) * flag_col[rows, :]
+            grad = gy[rows, :].astype(F32) * flag_col[rows, 0:1]
             n = normed[rows, :]
             dz = norm_back(grad * norm[4:5, :], n, inv[1, rows, :])
             wide[rows, :] = dz
@@ -1301,6 +1380,7 @@
         return link.send(spot, spot, place.core)
 
     got["small"].wait()
+    unpack_small(packed, small)
     norm_vectors(small, norm)
     reds[...] = jnp.zeros_like(reds)
     red_up[...] = jnp.zeros_like(red_up)
@@ -1308,13 +1388,22 @@
     small_grad[...] = jnp.zeros_like(small_grad)
     for name in ("normed", "gy", "inv"):
         got[name].wait()
+    load_ffn(0)
+    load("h", h_in, h_low)
     norm_two_back()
+    load_ffn(1)
     down = [(3, k) for k in steps]
     up = [(2, k) for k in steps]
     out = [(1, k) for k in steps]
     att_in_w = [(0, k) for k in steps]
     down_piece(0)
+    load("att", att_in, att)
+    load("wout", w_out, v_out)
+    load("qkvs", qkv_in, qkv)
     act_back(0)
+    load("x", x_in, x_row)
+    load_att(0)
+    load_att(1)
     core_add(*down[0])
     up_piece(0)
     hidden_back(0)
@@ -1396,9 +1485,11 @@
     row_loop(dx_body)
     for q in range(4):
         at = slice(192 * q, 192 * q + 192)
-        small_grad[q, 0:1, :] = jnp.concatenate(
+        line = jnp.concatenate(
             [red_qv[q], red_up[q]] + [reds[i : i + 1, at] for i in range(6)], axis=1
         )
+        for i in range(6):
+            small_grad[q, i : i + 1, :] = line[:, 384 * i : 384 * i + 384]
     small_sum = small_land.at[6]
     small_keep = link.copy(small_grad.at[t], small_sum)
     small_moves = [link.send(small_grad.at[t_of[k]], small_land.at[k - 1], place.deep[k]) for k in (1, 2, 3)]
@@ -1454,9 +1545,10 @@
         ((2, 384, 576), BF),
         ((96, 2304), F32),
         ((96, 2304), BF),
-        ((4, 8, 2304), F32),
-        ((11, 8, 2304), F32),
-        ((4, 8, 2304), F32),
+        ((4, 8, 384), F32),
+        ((11, 8, 384), F32),
+        ((4, 8, 384), F32),
+        ((4, 1, 2304), F32),
         ((8, 768), F32),
         ((512, 768), BF),
         ((512, 768), F32),
@@ -1483,13 +1575,14 @@
         ((8, 768), F32),
         ((4, 1, 768), F32),
         ((4, 1, 384), F32),
+        ((512, 8), F32),
     ]
     scratch = sums + sums + halves + halves + singles + singles + deeps + rest
     return pl.pallas_call(
         backward_kernel,
         out_shape=[
             shape((8, 96, 2304), BF),
-            shape((8, 2304), F32),
+            shape((8, 384), F32),
             shape((4, 128, 768), BF),
             shape((4, 128, 768), BF),
             shape((4, 8, 768), F32),
@@ -1509,6 +1602,106 @@
     )(*args)
 
 
+def finish_kernel(
+    slot_row,
+    blocks,
+    small,
+    pool,
+    master,
+    first,
+    second,
+    out_mine,
+    dx_mine,
+    new_master,
+    new_first,
+    new_second,
+    layer_out,
+    input_grad,
+    pooled,
+    norm_grads,
+):
+    step = pl.program_id(0)
+    rows = master.shape[0]
+    t = lax.axis_index("tensor")
+    start = lax.axis_index("dp") * (rows * pl.num_programs(0)) + step * rows
+    wanted = (lax.broadcasted_iota(jnp.int32, (rows, 1), 0) + start).astype(F32)
+    match = slot_row[0:1, :768] == wanted
+    gradient = dot_f32(jnp.where(match, 1.0, 0.0).astype(BF), blocks[...])
+    is_small = slot_row[0:1, 768:769] == wanted
+    small_line = jnp.concatenate([small[i : i + 1, :] for i in range(6)], axis=1)
+    gradient = jnp.where(is_small, small_line, gradient)
+
+    at = lax.broadcasted_iota(jnp.int32, (1, 768), 1) % 96
+    rates = jnp.where(
+        at < 32,
+        MODEL_WIDTH ** (-0.5),
+        jnp.where(
+            at < 64,
+            FF ** (-0.5),
+            jnp.where(at < 88, MODEL_WIDTH ** (-0.5), 4.0 * MODEL_WIDTH ** (-0.5)),
+        ),
+    ).astype(F32)
+    rate = jnp.sum(jnp.where(match, rates, 0.0), axis=1, keepdims=True)
+    filled = (rate > 0.0) | is_small
+    offset = lax.broadcasted_iota(jnp.int32, (1, small_line.shape[1]), 1) - 1152
+    gain = ((offset >= 384) & (offset < 576)) | ((offset >= 768) & (offset < 960))
+    small_rate = jnp.where(gain, 0.2, 0.1).astype(F32)
+    step_rate = jnp.where(is_small, small_rate, rate)
+    decay_on = jnp.where(is_small, 0.0, 1.0)
+    new_master[...], new_first[...], new_second[...] = adamw(
+        gradient, first[...], second[...], master[...], step_rate, decay_on, filled
+    )
+    for src, dst in ((out_mine, layer_out), (dx_mine, input_grad)):
+        for row in range(4):
+            dst[:, row, :] = src[row].astype(F32)
+
+    @pl.when(step == 0)
+    def _():
+        total = jnp.zeros((4, 8, 192), F32)
+        for q in range(4):
+            total = total + jnp.where(t == q, pool[:, :, 192 * q : 192 * q + 192], 0.0)
+        pooled[...] = total
+        norm_grads[...] = jnp.concatenate(
+            [small_line[:, 1152 + 192 * i : 1344 + 192 * i] for i in range(6)], axis=0
+        )
+
+
+def finish_call(slot_row, blocks, small, pool, master, first, second, out_mine, dx_mine):
+    steps = 4
+    slots, block_len = master.shape
+    shape = jax.ShapeDtypeStruct
+
+    def whole(*dims):
+        return pl.BlockSpec(dims, lambda i: (0,) * len(dims))
+
+    state = pl.BlockSpec((slots // steps, block_len), lambda i: (i, 0))
+    token_in = pl.BlockSpec((4, 128 // steps, 768), lambda i: (0, i, 0))
+    token_out = pl.BlockSpec((128 // steps, 4, 768), lambda i: (i, 0, 0))
+    return pl.pallas_call(
+        finish_kernel,
+        grid=(steps,),
+        out_shape=[shape((slots, block_len), F32)] * 3
+        + [shape((128, 4, 768), F32)] * 2
+        + [shape((4, 8, 192), F32), shape((6, 192), F32)],
+        in_specs=[whole(8, 896), whole(768, block_len), whole(8, 384), whole(4, 8, 768)]
+        + [state] * 3
+        + [token_in] * 2,
+        out_specs=[state] * 3 + [token_out] * 2 + [whole(4, 8, 192), whole(6, 192)],
+        compiler_params=pltpu.CompilerParams(vmem_limit_bytes=62 * MIB),
+        name="owners_update",
+    )(slot_row, blocks, small, pool, master, first, second, out_mine, dx_mine)
+
+
+def share_order():
+    order = []
+    for core in range(2):
+        for chip in range(4):
+            for base, count in ((0, 32), (256, 32), (512, 24), (704, 8)):
+                at = base + (core * 4 + chip) * count
+                order += list(range(at, at + count))
+    return np.array(order + [768] + [4096] * 127, np.int32)
+
+
 def local_rows(
     layer_input_rows,
     sentence_index_row,
@@ -1519,32 +1712,15 @@
     first_moment,
     second_moment,
 ):
-    tensor_at = lax.axis_index("tensor")
-    data_at = lax.axis_index("dp")
-    per_owner = master_state.shape[1]
     block_len = master_state.shape[2]
-    slot_of = slot_tables(owner_rank, per_owner)
-    slot_order = jnp.concatenate(
-        [
-            slot_of[:256].reshape(2, 4, 32),
-            slot_of[256:512].reshape(2, 4, 32),
-            slot_of[512:704].reshape(2, 4, 24),
-            slot_of[704:768].reshape(2, 4, 8),
-        ],
-        axis=2,
-    ).reshape(768)
-    core_order = lax.dynamic_slice_in_dim(slot_order, (data_at % 2) * 384, 384, 0)[:, None]
-    small_slot = jnp.broadcast_to(slot_of[768], (8, 1))
-
-    labels = lax.dynamic_index_in_dim(sentence_index_row, tensor_at, 0, keepdims=False)
-    flags = lax.dynamic_index_in_dim(padding_mask, tensor_at, 0, keepdims=False)
-    ids = jnp.where(flags == 1, labels, -1 - jnp.arange(flags.shape[0], dtype=jnp.int32))
+    order = share_order()
     (
         w_qkv,
         _,
         w_up,
         w_down,
         w_out,
+        slot_row,
         small_all,
         x_row,
         gy_row,
@@ -1561,15 +1737,15 @@
         pool_mean,
     ) = forward_call(
         master_state[0],
-        core_order,
-        small_slot,
-        ids[:, None],
-        ids[None],
+        owner_rank[None],
+        jnp.asarray(order[:, None]),
+        sentence_index_row,
+        padding_mask,
         jnp.transpose(layer_input_rows, (1, 0, 2)),
         jnp.transpose(output_gradient, (1, 0, 2)),
     )
     blocks, small_sum, out_mine, dx_mine, pool_all = backward_call(
-        flags.astype(F32)[:, None],
+        padding_mask,
         out_row,
         pool_mean,
         gy_row,
@@ -1589,30 +1765,21 @@
         w_qkv,
         x_row,
     )
-    small_row = small_sum[0]
-    norm_grads = small_row[1152:].reshape(6, 192)
-    pooled = lax.dynamic_slice_in_dim(pool_all, tensor_at * 192, 192, 2)
-
-    wanted = data_at * per_owner + jnp.arange(per_owner, dtype=jnp.int32)
-    block_of, filled = slot_blocks(slot_of, wanted)
-    pick = (slot_order[None, :] == wanted[:, None]).astype(BF)
-    owned = dot_f32(pick, blocks.reshape(768, block_len))
-    owned = jnp.where((wanted == slot_of[768])[:, None], small_row[None], owned)
-    token_position = block_of[:, None] * block_len + jnp.arange(block_len, dtype=jnp.int32)[None, :]
-    step_rate, decay_on = step_rates(token_position, MODEL_WIDTH, FF, 4)
-    new_master, new_first, new_second = adamw(
-        owned,
+    new_master, new_first, new_second, layer_out, input_grad, pooled, norm_grads = finish_call(
+        slot_row,
+        blocks.reshape(768, block_len),
+        small_sum,
+        pool_all,
+        master_state[0],
         first_moment[0],
         second_moment[0],
-        master_state[0],
-        step_rate,
-        decay_on,
-        filled[:, None],
+        out_mine,
+        dx_mine,
     )
     return (
-        jnp.transpose(out_mine, (1, 0, 2)).astype(F32),
+        layer_out,
         pooled,
-        jnp.transpose(dx_mine, (1, 0, 2)).astype(F32),
+        input_grad,
         new_master[None],
         new_first[None],
         new_second[None],

time: 263 us -> 239 us (0.909)
  local copies, waits for them, and re-layouts: 14.7 us -> 3.98 us
  other arithmetic: 7.41 us -> 0 us
  matrix products: 5.25 us -> 0 us
    pallas_call x0 -> x1, Pallas kernels: none -> 9.77 us  [finish_call(): pl.pallas_call(finish_kernel, grid=(steps,), out_shape=[shape((slots, blo...]
    pallas_call x1, Pallas kernels: 116 us -> 109 us  [backward_call(): pl.pallas_call(backward_kernel, out_shape=[shape((8, 96, 2304), BF), shap...]
    dot_general x1 -> x0, matrix products: 5.25 us -> none  [dot_f32(): return jnp.dot(a, b, preferred_element_type=F32)]
    unnamed x16 -> x0, local copies, waits for them, and re-layouts: 5.17 us -> none
    pallas_call x1, Pallas kernels: 114 us -> 111 us  [forward_call(): pl.pallas_call(forward_kernel, out_shape=[shape(*o) for o in outs], in_sp...]
where the time goes in v3:
time: 239 us; the launch traced here: 235 us
  Pallas kernels  230 us (96%)
  local copies, waits for them, and re-layouts  3.98 us (2%)
    pallas_call x1, Pallas kernels, forward_call(): pl.pallas_call(forward_kernel, out_shape=[shape(*o) for o in outs], in_sp...  111 us
    pallas_call x1, Pallas kernels, backward_call(): pl.pallas_call(backward_kernel, out_shape=[shape((8, 96, 2304), BF), shap...  109 us
    pallas_call x1, Pallas kernels, finish_call(): pl.pallas_call(finish_kernel, grid=(steps,), out_shape=[shape((slots, blo...  9.77 us

profile of v3, /device:TPU:9, one launch (start us, length us, event | category | flops | bytes accessed | tf_op | source)
XLA Modules:
  0.0 234.7 jit_solution(17852132898521984964)
XLA Ops:
  0.6 1.3 broadcast_in_dim.12.owners
  1.9 2.7 %copy_bitcast_fusion = (bf16[4,128,768]{2,1,0:T(8,128)(2,1)}, bf16[4,128,768]{2,1,0:T(8,128)(2,1)}) fusion(bf16[128,4,768]{2,1,0:T(4,128)(2,1)} %param.12, bf16[128,4,768]{2,1,0:T(4,128)(2,1)} %param.9), kind=kLoop, calls=%fused_computation | loop fusion | bytes 3145728 | tf_op jit(solution)/shard_map/transpose | solution.py:1745
  4.6 110.6 %gather_and_forward.1 = (bf16[4,768,576]{2,1,0:T(8,128)(2,1)}, bf16[4,256,768]{2,1,0:T(8,128)(2,1)}, bf16[4,768,768]{2,1,0:T(8,128)(2,1)}, bf16[4,768,768]{2,1,0...) custom-call(f32[192,2304]{1,0:T(8,128)} %bitcast.11, ...), custom_call_target="tpu_custom_call" | custom-call | tf_op jit(solution)/shard_map/gather_and_forward/pallas_call | solution.py:1011
  115.3 109.4 %backward_and_reduce.1 = (bf16[8,96,2304]{2,1,0:T(8,128)(2,1)}, f32[8,384]{1,0:T(8,128)}, bf16[4,128,768]{2,1,0:T(8,128)(2,1)}, bf16[4,128,768]{2,1,0:T(8,128)(2,1)}, f32[4,8,768]{2,1,0:T(8,128)}) custom-call(s32[4,512]{1,0:T(4,128)} %flags.3, bf16[512,768]{1,0:T(8,128)(2,1)} %get-tuple-element.39.out_row, f32[8,768]{1,0:T(8,128)} %get-tuple-element.40.pool_in, ...), custom_call_target="tpu_custom_call" | custom-call | tf_op jit(solution)/shard_map/backward_and_reduce/pallas_call | solution.py:1581
  224.7 9.8 %owners_update.1 = (f32[192,2304]{1,0:T(8,128)}, f32[192,2304]{1,0:T(8,128)}, f32[192,2304]{1,0:T(8,128)}, f32[128,4,768]{2,1,0:T(4,128)}, f32[128,4,768]{2,1,0:...) custom-call(f32[8,896]{1,0:T(8,128)} %get-tuple-element.38.slot_row, bf16[768,2304]{1,0:T(8,128)(2,1)} %bitcast.13, ...), custom_call_target="tpu_custom_call" | custom-call | tf_op jit(solution)/shard_map/owners_update/pallas_call | solution.py:1680

commit v4 on v3

--- a/solution.py
+++ b/solution.py
@@ -832,108 +832,138 @@
 
     every = range(4)
     others = (1, 2, 3)
-    deep_send(0)
-    plane_send(0, 0)
+    small_state, gy_moves = {}, []
+
+    def small_collect():
+        for move in small_moves:
+            move.wait_recv()
+        small_total[...] = small_mine[...] + small_land[0] + small_land[1] + small_land[2]
+        small_state["stay"] = link.copy(small_total, packed.at[place.t])
+        small_state["deep"] = [
+            link.send(small_total, packed.at[place.t], place.deep[k]) for k in others
+        ]
+
+    def small_ready():
+        small_state["stay"].wait()
+        for move in small_state["deep"]:
+            move.wait_recv()
+        unpack_small(packed, small)
+        norm_vectors(small, norm)
+        for t in every:
+            bias_qkv[t] = jnp.concatenate(
+                [small[t, 0:1, :192], jnp.zeros((1, 192), F32), small[t, 0:1, 192:384]], axis=1
+            )
+        tidy.append(link.copy(packed, small_out))
+
+    def x_ready():
+        x_stay.wait()
+        for move in x_moves:
+            move.wait_recv()
+        tidy.append(link.copy(x_row, x_out))
+
+    def gy_send():
+        for k in others:
+            gy_moves.append(link.send(gy_in.at[place.ahead[k]], gy_row.at[mine_rows], place.deep[k]))
+
+    def gy_ready():
+        for move in gy_moves:
+            move.wait_recv()
+
     spread_out()
     deep_send(1)
+    plane_send(0, 0)
+    pass_halves()
+    deep_send(0)
     plane_send(1, 0)
-    pass_halves()
+    plane_pass(0, 0)
+    plane_send(1, 3)
+    x_ready()
     collect_halves()
     spread_ffn()
     plane_send(2, 0)
-    plane_pass(0, 0)
-    for k in others:
-        plane_send(0, k)
+    small_collect()
+    plane_send(1, 2)
+    plane_send(0, 1)
+    plane_pass(1, 0)
     deep_send(2)
-    for move in small_moves:
-        move.wait_recv()
-    small_total[...] = small_mine[...] + small_land[0] + small_land[1] + small_land[2]
-    small_stay = link.copy(small_total, packed.at[place.t])
-    small_deep = [link.send(small_total, packed.at[place.t], place.deep[k]) for k in others]
-    x_stay.wait()
-    for move in x_moves:
-        move.wait_recv()
-    tidy.append(link.copy(x_row, x_out))
-    plane_pass(1, 0)
-    for k in others:
-        plane_send(1, k)
+    plane_send(1, 1)
+    plane_send(0, 3)
+    small_ready()
+    plane_pass(1, 3)
+    plane_pass(0, 1)
     core_pass(0, 0)
+    load(0, 0)
+    core_pass(1, 0)
+    plane_pass(1, 2)
+    plane_pass(0, 3)
+    core_pass(1, 3)
+    plane_pass(2, 0)
+    plane_send(0, 2)
+    deep_send(3)
+    core_pass(0, 1)
+    qkv_step(0)
+    load(0, 1)
+    plane_send(2, 1)
+    core_pass(0, 3)
+    attention(0)
+    load(0, 3)
+    qkv_step(3)
+    plane_send(2, 2)
+    load(1, 3)
+    gy_send()
+    qkv_step(1)
+    plane_pass(1, 1)
+    plane_pass(0, 2)
+    plane_send(2, 3)
+    core_pass(1, 2)
+    attention(3)
+    core_pass(1, 1)
     plane_send(3, 0)
-    for k in others:
-        plane_pass(0, k)
-    small_stay.wait()
-    for move in small_deep:
-        move.wait_recv()
-    unpack_small(packed, small)
-    norm_vectors(small, norm)
-    for t in every:
-        bias_qkv[t] = jnp.concatenate(
-            [small[t, 0:1, :192], jnp.zeros((1, 192), F32), small[t, 0:1, 192:384]], axis=1
-        )
-    tidy.append(link.copy(packed, small_out))
-    load(0, 0)
-    qkv_step(0)
-    attention(0)
-    for k in others:
-        plane_send(2, k)
-    deep_send(3)
-    for k in others:
-        plane_pass(1, k)
-        core_pass(0, k)
-    plane_pass(2, 0)
-    for k in others:
-        load(0, k)
-    qkv_step(1)
+    core_pass(0, 2)
+    core_pass(2, 0)
+    load(1, 0)
     attention(1)
+    plane_pass(2, 3)
+    plane_pass(2, 2)
+    plane_pass(2, 1)
+    load(1, 2)
+    plane_send(3, 2)
+    load(2, 0)
+    load(0, 2)
+    qkv_step(2)
+    load(1, 1)
     plane_pass(3, 0)
-    for k in every:
-        core_pass(1, k)
-    plane_pass(2, 1)
-    qkv_step(2)
+    plane_send(3, 3)
     attention(2)
-    plane_pass(2, 2)
-    core_pass(2, 0)
-    for k in every:
-        load(1, k)
-    qkv_step(3)
-    plane_pass(2, 3)
+    plane_send(3, 1)
+    core_pass(2, 3)
+    out_step()
+    load(2, 3)
     core_pass(2, 1)
-    attention(3)
-    load(2, 0)
-    plane_send(3, 1)
-    plane_send(3, 2)
-    plane_send(3, 3)
-    gy_moves = [
-        link.send(gy_in.at[place.ahead[k]], gy_row.at[mine_rows], place.deep[k]) for k in others
-    ]
+    up_step(0)
+    load(2, 1)
     core_pass(2, 2)
+    up_step(3)
+    plane_pass(3, 2)
+    load(2, 2)
     core_pass(3, 0)
-    out_step()
-    load(2, 1)
-    load(2, 2)
+    up_step(1)
     load(3, 0)
-    core_pass(2, 3)
+    plane_pass(3, 3)
+    up_step(2)
     plane_pass(3, 1)
-    up_step(0)
-    up_step(1)
-    plane_pass(3, 2)
-    core_pass(3, 1)
-    load(2, 3)
-    load(3, 1)
-    up_step(2)
-    plane_pass(3, 3)
     core_pass(3, 2)
-    up_step(3)
     down_step(0)
     core_pass(3, 3)
+    load(3, 2)
+    core_pass(3, 1)
+    load(3, 3)
+    down_step(2)
+    gy_ready()
+    load(3, 1)
+    down_step(3)
     down_step(1)
-    load(3, 2)
-    down_step(2)
-    load(3, 3)
-    down_step(3)
     end_step()
-    for move in gy_moves:
-        move.wait_recv()
     for copy in tidy:
         copy.wait()
     link.finish()
@@ -1100,25 +1130,25 @@
     steps = (1, 2, 3, 0)
     got = {}
 
-    def load(name, src, dst):
+    def fetch(name, src, dst):
         got[name] = link.copy(src, dst)
 
-    load("small", small_in, packed)
-    load("normed", n_two_in, normed)
-    load("gy", gy_in, gy)
-    load("inv", inv_in, inv)
+    fetch("small", small_in, packed)
+    fetch("normed", n_two_in, normed)
+    fetch("gy", gy_in, gy)
+    fetch("inv", inv_in, inv)
 
     def load_ffn(i):
         t, slot = t_of[steps[i]], i % 2
-        load(("act", i), act_in.at[t], act.at[slot])
-        load(("down", i), w_down.at[t], v_down.at[slot])
-        load(("pull", i), pull_in.at[t], pull.at[slot])
-        load(("up", i), w_up.at[t], v_up.at[slot])
+        fetch(("act", i), act_in.at[t], act.at[slot])
+        fetch(("down", i), w_down.at[t], v_down.at[slot])
+        fetch(("pull", i), pull_in.at[t], pull.at[slot])
+        fetch(("up", i), w_up.at[t], v_up.at[slot])
 
     def load_att(i):
         t, slot = t_of[steps[i]], i % 2
-        load(("prob", i), prob_in.at[pl.ds(3 * t, 3)], prob.at[slot])
-        load(("qkv", i), w_qkv.at[t], v_qkv.at[slot])
+        fetch(("prob", i), prob_in.at[pl.ds(3 * t, 3)], prob.at[slot])
+        fetch(("qkv", i), w_qkv.at[t], v_qkv.at[slot])
 
     own_flags = flags[pl.ds(place.t, 1), :].astype(F32)
     flag_col[...] = jnp.transpose(jnp.broadcast_to(own_flags, (8, 512)))
@@ -1267,10 +1297,8 @@
             total[rows, :] += dot_nt(d_up[rows, :], v_up[slot])
 
         row_loop(body, 256)
-        if i + 2 < 4:
-            load_ffn(i + 2)
         if i == 1:
-            load("n_one", n_one_in, normed)
+            fetch("n_one", n_one_in, normed)
 
     def norm_one_back():
         got["n_one"].wait()
@@ -1351,33 +1379,36 @@
             total[rows, :] += dot_nt(d_qkv[rows, :], v_qkv[slot])
 
         row_loop(body, 256)
-        if i + 2 < 4:
-            load_att(i + 2)
+
+    sent, passed, across = {}, {}, {}
 
     def share_send(lo, hi):
         share_low[lo:hi, :] = share[lo:hi, :].astype(BF)
         mine = c * 4 + place.xy
         rows = pl.ds(lo, hi - lo)
-        return (
+        sent[lo] = (
             link.copy(share_low.at[rows], blocks.at[mine, rows]),
             link.send(share_low.at[rows], blocks.at[mine, rows], place.right),
             link.send(share_low.at[rows], blocks.at[mine, rows], place.down),
         )
 
-    def share_pass(sent, lo, hi):
+    def share_pass(lo, hi):
         half = (hi - lo) // 2
-        sent[1].wait_recv()
-        sent[2].wait_recv()
+        sent[lo][1].wait_recv()
+        sent[lo][2].wait_recv()
         one = blocks.at[c * 4 + place.right[0] // 2, pl.ds(lo, half)]
         two = blocks.at[c * 4 + place.down[0] // 2, pl.ds(lo + half, half)]
-        return link.send(one, one, place.down), link.send(two, two, place.right)
-
-    def share_across(sent, passed, lo, hi):
-        sent[0].wait()
-        passed[0].wait_recv()
-        passed[1].wait_recv()
+        passed[lo] = link.send(one, one, place.down), link.send(two, two, place.right)
+
+    def share_across(lo, hi):
+        sent[lo][0].wait()
+        passed[lo][0].wait_recv()
+        passed[lo][1].wait_recv()
         spot = blocks.at[pl.ds(c * 4, 4), pl.ds(lo, hi - lo)]
-        return link.send(spot, spot, place.core)
+        across[lo] = link.send(spot, spot, place.core)
+
+    def share_ready(lo):
+        across[lo].wait_recv()
 
     got["small"].wait()
     unpack_small(packed, small)
@@ -1388,143 +1419,165 @@
     small_grad[...] = jnp.zeros_like(small_grad)
     for name in ("normed", "gy", "inv"):
         got[name].wait()
+    def load_rest():
+        fetch("h", h_in, h_low)
+        fetch("att", att_in, att)
+        fetch("wout", w_out, v_out)
+        fetch("qkvs", qkv_in, qkv)
+        fetch("x", x_in, x_row)
+
+    small_state = {}
+
+    def small_send():
+        def dx_body(rows):
+            low[rows, :] = total[rows, :].astype(BF)
+
+        row_loop(dx_body)
+        for q in range(4):
+            at = slice(192 * q, 192 * q + 192)
+            line = jnp.concatenate(
+                [red_qv[q], red_up[q]] + [reds[i : i + 1, at] for i in range(6)], axis=1
+            )
+            for i in range(6):
+                small_grad[q, i : i + 1, :] = line[:, 384 * i : 384 * i + 384]
+        small_state["keep"] = link.copy(small_grad.at[t], small_land.at[6])
+        small_state["deep"] = [
+            link.send(small_grad.at[t_of[k]], small_land.at[k - 1], place.deep[k]) for k in (1, 2, 3)
+        ]
+
+    def dx_send():
+        own_rows = pl.ds(pl.multiple_of(t * 128, 128), 128)
+        stay.append(link.copy(low.at[own_rows], dx_mine.at[t]))
+        for k in (1, 2, 3):
+            part = low.at[pl.ds(pl.multiple_of(t_of[k] * 128, 128), 128)]
+            moves.append(link.send(part, dx_mine.at[t], place.deep[k]))
+
+    def small_core():
+        small_state["keep"].wait()
+        for move in small_state["deep"]:
+            move.wait_recv()
+        small_land[7] = small_land[6] + small_land[0] + small_land[1] + small_land[2]
+        small_state["core"] = link.send(small_land.at[7], small_land.at[3], place.core)
+
+    def small_right():
+        small_state["core"].wait_recv()
+        small_land[8] = small_land[7] + small_land[3]
+        small_state["right"] = link.send(small_land.at[8], small_land.at[4], place.right)
+
+    def small_down():
+        small_state["right"].wait_recv()
+        small_land[9] = small_land[8] + small_land[4]
+        small_state["down"] = link.send(small_land.at[9], small_land.at[5], place.down)
+
+    def small_end():
+        small_state["down"].wait_recv()
+        small_out[...] = small_land[9] + small_land[5]
+
     load_ffn(0)
-    load("h", h_in, h_low)
     norm_two_back()
     load_ffn(1)
-    down = [(3, k) for k in steps]
-    up = [(2, k) for k in steps]
-    out = [(1, k) for k in steps]
-    att_in_w = [(0, k) for k in steps]
     down_piece(0)
-    load("att", att_in, att)
-    load("wout", w_out, v_out)
-    load("qkvs", qkv_in, qkv)
+    load_rest()
     act_back(0)
-    load("x", x_in, x_row)
+    core_add(3, 1)
     load_att(0)
     load_att(1)
-    core_add(*down[0])
     up_piece(0)
     hidden_back(0)
-    core_add(*up[0])
-    plane_add(*down[0])
+    load_ffn(2)
+    core_add(2, 1)
     down_piece(1)
     act_back(1)
-    core_add(*down[1])
-    plane_add(*up[0])
+    core_add(3, 2)
     up_piece(1)
-    deep_add(*down[0])
     hidden_back(1)
-    core_add(*up[1])
-    plane_add(*down[1])
+    core_add(2, 2)
+    load_ffn(3)
     down_piece(2)
-    deep_add(*up[0])
     act_back(2)
-    core_add(*down[2])
+    plane_add(3, 2)
+    plane_add(3, 1)
     up_piece(2)
-    plane_add(*up[1])
-    deep_add(*down[1])
     hidden_back(2)
-    core_add(*up[2])
     down_piece(3)
-    plane_add(*down[2])
-    deep_add(*up[1])
+    plane_add(2, 2)
+    core_add(2, 3)
     act_back(3)
-    core_add(*down[3])
+    plane_add(2, 1)
     up_piece(3)
-    deep_add(*down[2])
+    deep_add(3, 2)
     hidden_back(3)
-    core_add(*up[3])
-    plane_add(*up[2])
+    deep_add(2, 2)
     norm_one_back()
+    core_add(3, 3)
     out_piece(0)
-    plane_add(*down[3])
-    deep_add(*up[2])
+    core_add(2, 0)
     attention_back(0)
-    core_add(*out[0])
-    plane_add(*up[3])
-    deep_add(*down[3])
+    deep_add(2, 1)
     qkv_piece(0)
+    plane_add(2, 3)
+    load_att(2)
+    core_add(0, 1)
+    deep_add(3, 1)
     out_piece(1)
-    deep_add(*up[3])
-    core_add(*att_in_w[0])
     attention_back(1)
-    core_add(*out[1])
-    plane_add(*out[0])
+    plane_add(3, 3)
+    core_add(1, 2)
+    plane_add(2, 0)
+    deep_add(2, 3)
+    qkv_piece(1)
+    load_att(3)
+    out_piece(2)
+    plane_add(0, 1)
+    attention_back(2)
+    core_add(0, 2)
+    deep_add(3, 3)
+    core_add(1, 1)
+    qkv_piece(2)
+    deep_add(0, 1)
+    out_piece(3)
+    plane_add(1, 2)
+    core_add(1, 3)
+    core_add(0, 3)
+    attention_back(3)
+    deep_add(1, 2)
+    plane_add(0, 2)
+    plane_add(1, 3)
+    core_add(1, 0)
+    plane_add(1, 1)
+    plane_add(0, 3)
+    core_add(3, 0)
+    deep_add(0, 2)
+    qkv_piece(3)
+    small_send()
+    core_add(0, 0)
+    deep_add(0, 3)
+    deep_add(1, 1)
+    deep_add(1, 3)
+    plane_add(3, 0)
+    small_core()
+    deep_add(2, 0)
+    end(2)
+    plane_add(1, 0)
+    dx_send()
+    plane_add(0, 0)
+    small_right()
+    deep_add(3, 0)
     end(3)
-    end(2)
-    ffn_sent = share_send(0, 64)
-    qkv_piece(1)
-    plane_add(*att_in_w[0])
-    deep_add(*out[0])
-    out_piece(2)
-    core_add(*att_in_w[1])
-    attention_back(2)
-    core_add(*out[2])
-    plane_add(*out[1])
-    deep_add(*att_in_w[0])
-    ffn_passed = share_pass(ffn_sent, 0, 64)
-    qkv_piece(2)
-    plane_add(*att_in_w[1])
-    out_piece(3)
-    core_add(*att_in_w[2])
-    deep_add(*out[1])
-    attention_back(3)
-    core_add(*out[3])
-    plane_add(*out[2])
-    deep_add(*att_in_w[1])
-    qkv_piece(3)
-    plane_add(*att_in_w[2])
-    plane_add(*out[3])
-    core_add(*att_in_w[3])
-
-    def dx_body(rows):
-        low[rows, :] = total[rows, :].astype(BF)
-
-    row_loop(dx_body)
-    for q in range(4):
-        at = slice(192 * q, 192 * q + 192)
-        line = jnp.concatenate(
-            [red_qv[q], red_up[q]] + [reds[i : i + 1, at] for i in range(6)], axis=1
-        )
-        for i in range(6):
-            small_grad[q, i : i + 1, :] = line[:, 384 * i : 384 * i + 384]
-    small_sum = small_land.at[6]
-    small_keep = link.copy(small_grad.at[t], small_sum)
-    small_moves = [link.send(small_grad.at[t_of[k]], small_land.at[k - 1], place.deep[k]) for k in (1, 2, 3)]
-
-    deep_add(*out[2])
-    deep_add(*att_in_w[2])
-    own_rows = pl.ds(pl.multiple_of(t * 128, 128), 128)
-    stay.append(link.copy(low.at[own_rows], dx_mine.at[t]))
-    for k in (1, 2, 3):
-        part = low.at[pl.ds(pl.multiple_of(t_of[k] * 128, 128), 128)]
-        moves.append(link.send(part, dx_mine.at[t], place.deep[k]))
-    small_keep.wait()
-    for move in small_moves:
-        move.wait_recv()
-    small_land[7] = small_land[6] + small_land[0] + small_land[1] + small_land[2]
-    doubling = [link.send(small_land.at[7], small_land.at[3], place.core)]
-    deep_add(*out[3])
-    plane_add(*att_in_w[3])
-    ffn_across = share_across(ffn_sent, ffn_passed, 0, 64)
-    deep_add(*att_in_w[3])
+    share_send(0, 64)
+    deep_add(0, 0)
+    end(0)
+    deep_add(1, 0)
     end(1)
-    doubling[0].wait_recv()
-    small_land[8] = small_land[7] + small_land[3]
-    doubling.append(link.send(small_land.at[8], small_land.at[4], place.right))
-    end(0)
-    att_sent = share_send(64, 96)
-    doubling[1].wait_recv()
-    small_land[9] = small_land[8] + small_land[4]
-    doubling.append(link.send(small_land.at[9], small_land.at[5], place.down))
-    att_passed = share_pass(att_sent, 64, 96)
-    doubling[2].wait_recv()
-    small_out[...] = small_land[9] + small_land[5]
-    att_across = share_across(att_sent, att_passed, 64, 96)
-    ffn_across.wait_recv()
-    att_across.wait_recv()
+    share_send(64, 96)
+    share_pass(0, 64)
+    small_down()
+    share_pass(64, 96)
+    share_across(0, 64)
+    share_across(64, 96)
+    share_ready(0)
+    share_ready(64)
+    small_end()
     for move in moves:
         move.wait_recv()
     for copy in stay:

time: 239 us -> 221 us (0.925)
  the two profiles are of different devices: /device:TPU:9 before, /device:TPU:25 now
where the time goes in v4:
time: 221 us; the launch traced here: 217 us
  Pallas kernels  212 us (96%)
  local copies, waits for them, and re-layouts  3.98 us (2%)
    pallas_call x1, Pallas kernels, forward_call(): pl.pallas_call(forward_kernel, out_shape=[shape(*o) for o in outs], in_sp...  105 us
    pallas_call x1, Pallas kernels, backward_call(): pl.pallas_call(backward_kernel, out_shape=[shape((8, 96, 2304), BF), shap...  96.8 us
    pallas_call x1, Pallas kernels, finish_call(): pl.pallas_call(finish_kernel, grid=(steps,), out_shape=[shape((slots, blo...  9.77 us

profile of v4, /device:TPU:25, one launch (start us, length us, event | category | flops | bytes accessed | tf_op | source)
XLA Modules:
  0.0 216.6 jit_solution(11456669529031819200)
XLA Ops:
  0.6 1.3 broadcast_in_dim.12.owners
  1.9 2.7 %copy_bitcast_fusion = (bf16[4,128,768]{2,1,0:T(8,128)(2,1)}, bf16[4,128,768]{2,1,0:T(8,128)(2,1)}) fusion(bf16[128,4,768]{2,1,0:T(4,128)(2,1)} %param.12, bf16[128,4,768]{2,1,0:T(4,128)(2,1)} %param.9), kind=kLoop, calls=%fused_computation | loop fusion | bytes 3145728 | tf_op jit(solution)/shard_map/transpose | solution.py:1798
  4.6 105.2 %gather_and_forward.1 = (bf16[4,768,576]{2,1,0:T(8,128)(2,1)}, bf16[4,256,768]{2,1,0:T(8,128)(2,1)}, bf16[4,768,768]{2,1,0:T(8,128)(2,1)}, bf16[4,768,768]{2,1,0...) custom-call(f32[192,2304]{1,0:T(8,128)} %bitcast.11, ...), custom_call_target="tpu_custom_call" | custom-call | tf_op jit(solution)/shard_map/gather_and_forward/pallas_call | solution.py:1041
  109.8 96.8 %backward_and_reduce.1 = (bf16[8,96,2304]{2,1,0:T(8,128)(2,1)}, f32[8,384]{1,0:T(8,128)}, bf16[4,128,768]{2,1,0:T(8,128)(2,1)}, bf16[4,128,768]{2,1,0:T(8,128)(2,1)}, f32[4,8,768]{2,1,0:T(8,128)}) custom-call(s32[4,512]{1,0:T(4,128)} %flags.3, bf16[512,768]{1,0:T(8,128)(2,1)} %get-tuple-element.39.out_row, f32[8,768]{1,0:T(8,128)} %get-tuple-element.40.pool_in, ...), custom_call_target="tpu_custom_call" | custom-call | tf_op jit(solution)/shard_map/backward_and_reduce/pallas_call | solution.py:1634
  206.6 9.8 %owners_update.1 = (f32[192,2304]{1,0:T(8,128)}, f32[192,2304]{1,0:T(8,128)}, f32[192,2304]{1,0:T(8,128)}, f32[128,4,768]{2,1,0:T(4,128)}, f32[128,4,768]{2,1,0:...) custom-call(f32[8,896]{1,0:T(8,128)} %get-tuple-element.38.slot_row, bf16[768,2304]{1,0:T(8,128)(2,1)} %bitcast.13, ...), custom_call_target="tpu_custom_call" | custom-call | tf_op jit(solution)/shard_map/owners_update/pallas_call | solution.py:1733
